TPU v7x, 256 devices: a whole 4x4x8 slice. The times are simulated.
256 devices in a mesh: section: 16 (over z_lo, x, core), tensor: 4 (over z_hi), dp: 4 (over y).
Axes of the slice: x: 4, y: 4, z: 8 (z_hi: 4, z_lo: 2; z = z_hi * 2 + z_lo), core: 2. Of those that a mesh axis runs over, the one named last changes fastest.
Arguments:
- attn_a: bfloat16 [16, 512, 7168], P('section', 'dp', 'tensor'), may hold values from -15 to 15, as said below
- attn_b: bfloat16 [16, 512, 7168], P('section', 'dp', 'tensor'), may hold values from -15 to 15, as said below
- w_down: bfloat16 [16, 7168, 768], P('section', 'tensor'), may hold values from -0.0625 to 0.0625
- q_gain: bfloat16 [16, 768], P('section'), may hold values from 0.099609375 to 1.8984375
- w_up: bfloat16 [16, 768, 12288], P('section', None, 'tensor'), may hold values from -0.21875 to 0.21875
- dq_a: bfloat16 [16, 512, 12288], P('section', 'dp', 'tensor'), may hold values from -6 to 6
- dq_b: bfloat16 [16, 512, 12288], P('section', 'dp', 'tensor'), may hold values from -6 to 6
Outputs:
- grad_down: bfloat16 [16, 7168, 768], P('section', ('tensor', 'dp'))
- grad_gain: bfloat16 [16, 768], P('section', 'dp')
- grad_up: bfloat16 [16, 768, 12288], P('section', 'dp', 'tensor')
Inputs may be any that keep to these rules, and one draw needn't show every extreme that they name: attn_a is real-valued. attn_b is real-valued.
All inputs are finite; a program needn't handle non-finite values.
Results may differ from a plain program's by a relative error of at most 0.035.
Values may be sent and summed in bfloat16 or wider, within the bound.
A program may use at most 128 MiB of HBM per device.

v0:
```python
import jax
import jax.numpy as jnp
from jax import lax
from jax.sharding import PartitionSpec as P

EPSILON = 1e-06


def prefix(x, axis, combine, identity, reverse):
    count, mine = (lax.axis_size(axis), lax.axis_index(axis))
    everything = lax.all_gather(x.astype(jnp.bfloat16), axis)
    start = jnp.broadcast_to(jnp.asarray(identity, x.dtype), x.shape)

    def lap(k, before):
        at = count - 1 - k if reverse else k
        reached = at > mine if reverse else at < mine
        new = combine(before, everything[at].astype(x.dtype))
        return jnp.where(reached, new, before)

    return lax.fori_loop(0, count, lap, start)


def partner(x, axis, distance):
    return lax.ppermute(x, axis, [(i, i ^ 1 << distance) for i in range(lax.axis_size(axis))])


def section_norm(latent, gain_row):
    inverse = lax.rsqrt(jnp.mean(latent * latent, axis=-1, keepdims=True) + EPSILON)
    normed = (latent * inverse * gain_row).astype(jnp.bfloat16)
    return (normed, inverse)


def norm_back(grad_normed, latent, inverse, gain_row):
    scaled = grad_normed * gain_row
    grad_gain = jnp.sum(grad_normed * latent * inverse, axis=0)
    grad_latent = inverse * scaled - latent * inverse**3 * jnp.mean(
        scaled * latent, axis=-1, keepdims=True
    )
    return (grad_latent.astype(jnp.bfloat16), grad_gain)


def combine_sum(earlier, latter):
    return earlier + latter


def local(attn_a, attn_b, w_down, q_gain, w_up, dq_a, dq_b):
    own_a = attn_a[0].astype(jnp.float32)
    own_b = attn_b[0].astype(jnp.float32)
    zeros_block = jnp.zeros_like(own_a)
    lower_a = prefix(own_a, "section", combine_sum, zeros_block, False)
    upper_b = prefix(own_b, "section", combine_sum, zeros_block, True)
    hidden_b = (upper_b + own_b).astype(jnp.bfloat16)
    hidden_a = (lower_a + own_a).astype(jnp.bfloat16)
    down_local = w_down[0]
    gain_row = q_gain[0].astype(jnp.float32)
    up_local = w_up[0]
    query_grad_a = dq_a[0]
    query_grad_b = dq_b[0]
    section_bits = lax.axis_size("section").bit_length() - 1
    latent_a, latent_b = (
        lax.psum(
            jnp.dot(hidden_a, down_local, preferred_element_type=jnp.float32).astype(jnp.bfloat16),
            "tensor",
        ).astype(jnp.float32),
        lax.psum(
            jnp.dot(hidden_b, down_local, preferred_element_type=jnp.float32).astype(jnp.bfloat16),
            "tensor",
        ).astype(jnp.float32),
    )
    normed_a, inverse_a = section_norm(latent_a, gain_row)
    normed_b, inverse_b = section_norm(latent_b, gain_row)
    grad_up = jnp.einsum(
        "tq,th->qh", normed_a, query_grad_a, preferred_element_type=jnp.float32
    ) + jnp.einsum("tq,th->qh", normed_b, query_grad_b, preferred_element_type=jnp.float32)
    back_a, back_b = (
        lax.psum(
            jnp.einsum(
                "th,qh->tq", query_grad_a, up_local, preferred_element_type=jnp.float32
            ).astype(jnp.bfloat16),
            "tensor",
        ).astype(jnp.float32),
        lax.psum(
            jnp.einsum(
                "th,qh->tq", query_grad_b, up_local, preferred_element_type=jnp.float32
            ).astype(jnp.bfloat16),
            "tensor",
        ).astype(jnp.float32),
    )
    latent_grad_a, gain_part_a = norm_back(back_a, latent_a, inverse_a, gain_row)
    latent_grad_b, gain_part_b = norm_back(back_b, latent_b, inverse_b, gain_row)
    grad_downw = jnp.einsum(
        "td,tq->dq", hidden_a, latent_grad_a, preferred_element_type=jnp.float32
    ) + jnp.einsum("td,tq->dq", hidden_b, latent_grad_b, preferred_element_type=jnp.float32)
    grad_gainw = gain_part_a + gain_part_b
    down_shard, gain_shard, up_shard = (
        lax.psum_scatter(
            grad_downw.astype(jnp.bfloat16), "dp", scatter_dimension=0, tiled=True
        ).astype(jnp.float32),
        lax.psum_scatter(
            grad_gainw.astype(jnp.bfloat16), "dp", scatter_dimension=0, tiled=True
        ).astype(jnp.float32),
        lax.psum_scatter(
            grad_up.astype(jnp.bfloat16), "dp", scatter_dimension=0, tiled=True
        ).astype(jnp.float32),
    )
    down_shard = down_shard.astype(jnp.bfloat16)
    gain_shard = gain_shard.astype(jnp.bfloat16)
    up_shard = up_shard.astype(jnp.bfloat16)
    down_other, gain_other, up_other = (down_shard, gain_shard, up_shard)
    for bit_index in range(section_bits):
        down_other, gain_other, up_other = partner(
            (down_other, gain_other, up_other), "section", bit_index
        )
    up_result = (up_shard.astype(jnp.float32) + up_other.astype(jnp.float32)).astype(jnp.bfloat16)
    down_result = (down_shard.astype(jnp.float32) + down_other.astype(jnp.float32)).astype(
        jnp.bfloat16
    )
    gain_result = (gain_shard.astype(jnp.float32) + gain_other.astype(jnp.float32)).astype(
        jnp.bfloat16
    )
    return (down_result[None], gain_result[None], up_result[None])


def solution(mesh):
    return jax.shard_map(
        local,
        mesh=mesh,
        in_specs=(
            P("section", "dp", "tensor"),
            P("section", "dp", "tensor"),
            P("section", "tensor", None),
            P("section", None),
            P("section", None, "tensor"),
            P("section", "dp", "tensor"),
            P("section", "dp", "tensor"),
        ),
        out_specs=(
            P("section", ("tensor", "dp"), None),
            P("section", "dp"),
            P("section", "dp", "tensor"),
        ),
        check_vma=False,
    )
```

profile of v0, /device:TPU:1, one launch (start us, length us, event | category | flops | bytes accessed | tf_op | source)
XLA Modules:
  0.0 419.4 jit_solution(11855908433091307358)
XLA Ops:
  8.8 5.1 %fusion.15 = bf16[128,768]{1,0:T(8,128)(2,1)} fusion(bf16[1,768,3072]{2,1,0:T(8,128)(2,1)} %param.15, bf16[1,128,3072]{2,1,0:T(8,128)(2,1)} %param.16), kind=kOutput, calls=%fused_computation.17 | convolution fusion | flops 604078080 | bytes 5701632 | tf_op jit(solution)/shard_map/th,qh->tq/dot_general | solution.py:77
  16.2 47.7 %all-gather.3.cloned.1.call-done = bf16[16,128,1792]{2,1,0:T(8,128)(2,1)} async-done(((bf16[1,128,1792]{2,1,0:T(8,128)(2,1)}), bf16[16,128,1792]{2,1,0:T(8,128)(2,1)}) %all-gather.3.cloned.1.call-update) | async-done | bytes 7340048 | tf_op jit(solution)/shard_map/all_gather | solution.py:11
  63.9 37.4 %while.30 = (s32[]{:T(128)}, f32[128,1792]{1,0:T(8,128)}, s32[]{:T(128)}, bf16[16,128,1792]{2,1,0:T(8,128)(2,1)}, s32[]{:T(128)}, /*index=5*/s32[]{:T(128)}) while((s32[]{:T(128)}, f32[128,1792]{1,0:T(8,128)}, s32[]{:T(128)}, bf16[16,128,1792]{2,1,0:T(8,128)(2,1)}, s32[]{:T(128)}, /*index=5*/s32[]{:T(128)}) %tuple.78), condition=%wide.region_1.2_spmd.clone, body=%wide.region_0.1_spmd.clone.sunk | while | flops 917508 | bytes 2293861 | solution.py:20
  77.7 2.4 add_select_fusion.4
  82.4 2.4 add_select_fusion.4
  98.9 2.4 add_select_fusion.4
  101.3 15.1 %all-gather.5.cloned.1.call-done = bf16[16,128,1792]{2,1,0:T(8,128)(2,1)} async-done(((bf16[1,128,1792]{2,1,0:T(8,128)(2,1)}), bf16[16,128,1792]{2,1,0:T(8,128)(2,1)}) %all-gather.5.cloned.1.call-update) | async-done | bytes 7340048 | tf_op jit(solution)/shard_map/all_gather | solution.py:11
  116.4 37.5 %while.31 = (s32[]{:T(128)}, f32[128,1792]{1,0:T(8,128)}, s32[]{:T(128)}, bf16[16,128,1792]{2,1,0:T(8,128)(2,1)}, s32[]{:T(128)}, /*index=5*/s32[]{:T(128)}, s32[]{:T(128)}, s32[]{:T(128)}) while((s32[]{:T(128)}, f32[128,1792]{1,0:T(8,128)}, s32[]{:T(128)}, bf16[16,128,1792]{2,1,0:T(8,128)(2,1)}, s32[]{:T(128)}, ...), condition=%wide.region_7.8_spmd.clone, body=%wide.region_6.7_spmd.clone.sunk | while | flops 917512 | bytes 2293923 | solution.py:20
  154.0 2.5 fusion.9
  157.8 61.7 %all-reduce.4.cloned.1.call-done = (bf16[128,768]{1,0:T(8,128)(2,1)}, bf16[128,768]{1,0:T(8,128)(2,1)}, bf16[128,768]{1,0:T(8,128)(2,1)}, bf16[128,768]{1,0:T(8,128)(2,1)}) async-done(((bf16[128,768]{1,0:T(8,128)(2,1)}, bf16[128,768]{1,0:T(8,128)(2,1)}, bf16[128,768]{1,0:T(8,128)(2,1)}, bf16[128,768]{1,0:T(8,128)(2,1)}), (bf16[128,768]{1,0:T(8,128)(2,1)}, bf16[128,768]{1,0:T(8,128)(2,1)}, ...) | async-done | bytes 786448 | tf_op jit(solution)/shard_map/psum | solution.py:76
  220.8 2.8 fusion.25
  223.6 3.6 add_convert_fusion
  228.8 2.4 fusion.51
  231.3 2.6 add_convert_fusion.1
  233.8 45.9 %reduce-scatter.5.cloned.1.call-done = bf16[192,3072]{1,0:T(8,128)(2,1)} async-done(((bf16[768,3072]{1,0:T(8,128)(2,1)}), bf16[192,3072]{1,0:T(8,128)(2,1)}) %reduce-scatter.5.cloned.1.call-update) | async-done | bytes 1179664 | tf_op jit(solution)/shard_map/reduce_scatter | solution.py:102
  280.4 2.8 collective-permute-done.8
  284.4 35.2 %reduce-scatter.3.cloned.1.call-done = bf16[448,768]{1,0:T(8,128)(2,1)} async-done(((bf16[1792,768]{1,0:T(8,128)(2,1)}), bf16[448,768]{1,0:T(8,128)(2,1)}) %reduce-scatter.3.cloned.1.call-update) | async-done | bytes 688144 | tf_op jit(solution)/shard_map/reduce_scatter | solution.py:96
  320.2 2.7 collective-permute-start.10
  323.4 40.9 %collective-permute-done.1 = bf16[448,768]{1,0:T(8,128)(2,1)S(1)} collective-permute-done((bf16[448,768]{1,0:T(8,128)(2,1)S(1)}, bf16[448,768]{1,0:T(8,128)(2,1)S(1)}, u32[]{:S(2)}, u32[]{:S(2)}) %collective-permute-start.1) | collective-permute-done | bytes 688160 | tf_op jit(solution)/shard_map/ppermute | solution.py:24
  367.3 14.7 %collective-permute-done.2 = bf16[448,768]{1,0:T(8,128)(2,1)} collective-permute-done((bf16[448,768]{1,0:T(8,128)(2,1)S(1)}, bf16[448,768]{1,0:T(8,128)(2,1)}, u32[]{:S(2)}, u32[]{:S(2)}) %collective-permute-start.2) | collective-permute-done | bytes 688160 | tf_op jit(solution)/shard_map/ppermute | solution.py:24
  384.6 6.6 %all-reduce = bf16[768]{0:T(1024)(128)(2,1)S(1)} all-reduce(bf16[768]{0:T(1024)(128)(2,1)S(1)} %add_convert_fusion.4), channel_id=3, replica_groups=mesh['section'=16,'tensor'=4,'dp'=4] {'dp'}, use_global_device_ids=true, to_apply=%region_15.16.clone | all-reduce | flops 768 | bytes 3072
  391.2 4.0 collective-permute-start.4
  402.8 4.6 %collective-permute-done.7 = bf16[192]{0:T(256)(128)(2,1)S(1)} collective-permute-done((bf16[192]{0:T(256)(128)(2,1)S(1)}, bf16[192]{0:T(256)(128)(2,1)S(1)}, u32[]{:S(2)}, u32[]{:S(2)}) %collective-permute-start.7) | collective-permute-done | bytes 416 | tf_op jit(solution)/shard_map/ppermute | solution.py:24
  410.2 2.7 fusion.8
  (102 shorter events, 93.9 us)
Async XLA Ops:
  7.2 146.8 %copy-start = (bf16[1,1792,768]{2,1,0:T(8,128)(2,1)S(1)}, bf16[1,1792,768]{2,1,0:T(8,128)(2,1)}, u32[]{:S(2)}) copy-start(bf16[1,1792,768]{2,1,0:T(8,128)(2,1)} %param.13) | copy-start | bytes 8257540
  7.2 56.7 %all-gather.3.cloned.1.call-start = ((), (), s32[]{:S(2)}) async-start(), calls=%async_computation.2 | async-start | bytes 7798784 | tf_op jit(solution)/shard_map/all_gather | solution.py:11
  7.9 108.5 %all-gather.5.cloned.1.call-start = ((), (), s32[]{:S(2)}) async-start(), calls=%async_computation.3 | async-start | bytes 7798784 | tf_op jit(solution)/shard_map/all_gather | solution.py:11
  8.7 210.9 %all-reduce.4.cloned.1.call-start = ((), (), s32[]{:S(2)}) async-start(), calls=%async_computation.6 | async-start | bytes 1572864 | tf_op jit(solution)/shard_map/psum | solution.py:76
  8.7 5.1 %copy-start.3 = (bf16[1,768,3072]{2,1,0:T(8,128)(2,1)S(1)}, bf16[1,768,3072]{2,1,0:T(8,128)(2,1)}, u32[]{:S(2)}) copy-start(bf16[1,768,3072]{2,1,0:T(8,128)(2,1)} %param.15) | copy-start | bytes 14155780
  8.7 5.1 %copy-start.8 = (bf16[1,128,3072]{2,1,0:T(8,128)(2,1)S(1)}, bf16[1,128,3072]{2,1,0:T(8,128)(2,1)}, u32[]{:S(2)}) copy-start(bf16[1,128,3072]{2,1,0:T(8,128)(2,1)} %param.17) | copy-start | bytes 2359300
  116.4 37.6 %copy-start.4 = (bf16[1,128,1792]{2,1,0:T(8,128)(2,1)S(1)}, bf16[1,128,1792]{2,1,0:T(8,128)(2,1)}, u32[]{:S(2)}) copy-start(bf16[1,128,1792]{2,1,0:T(8,128)(2,1)} %param.11) | copy-start | bytes 1376260
  157.8 122.0 %reduce-scatter.5.cloned.1.call-start = ((), (), s32[]{:S(2)}) async-start(), calls=%async_computation.5 | async-start | bytes 5898240 | tf_op jit(solution)/shard_map/reduce_scatter | solution.py:102
  220.8 2.8 copy-start.7
  227.3 92.3 %reduce-scatter.3.cloned.1.call-start = ((), (), s32[]{:S(2)}) async-start(), calls=%async_computation.4 | async-start | bytes 3440640 | tf_op jit(solution)/shard_map/reduce_scatter | solution.py:96
  233.8 149.5 %copy-start.13 = (u32[256]{0:T(256)S(1)}, u32[256]{0:T(256)}, u32[]{:S(2)}) copy-start(u32[256]{0:T(256)} %constant.91) | copy-start | bytes 3076
  279.8 3.4 collective-permute-start.8
  283.2 37.0 %collective-permute-start.9 = (bf16[192,3072]{1,0:T(8,128)(2,1)}, bf16[192,3072]{1,0:T(8,128)(2,1)}, u32[]{:S(2)}, u32[]{:S(2)}) collective-permute-start(bf16[192,3072]{1,0:T(8,128)(2,1)} %collective-permute-done.8), channel_id=1, source_target_pairs={{0,32},{16,48},{32,0},{48,16},{64,96},{80,112},{96,64},{112,80},{1... | collective-permute-start | bytes 3538952 | tf_op jit(solution)/shard_map/ppermute | solution.py:24
  319.6 3.3 collective-permute-start
  320.2 45.9 %collective-permute-start.10 = (bf16[192,3072]{1,0:T(8,128)(2,1)}, bf16[192,3072]{1,0:T(8,128)(2,1)}, u32[]{:S(2)}, u32[]{:S(2)}) collective-permute-start(bf16[192,3072]{1,0:T(8,128)(2,1)} %collective-permute-done.9), channel_id=1, source_target_pairs={{0,64},{16,80},{32,96},{48,112},{64,0},{80,16},{96,32},{112,48},{1... | collective-permute-start | bytes 3538952 | tf_op jit(solution)/shard_map/ppermute | solution.py:24
  322.9 41.4 %collective-permute-start.1 = (bf16[448,768]{1,0:T(8,128)(2,1)S(1)}, bf16[448,768]{1,0:T(8,128)(2,1)S(1)}, u32[]{:S(2)}, u32[]{:S(2)}) collective-permute-start(bf16[448,768]{1,0:T(8,128)(2,1)S(1)} %collective-permute-done), channel_id=1, source_target_pairs={{0,32},{16,48},{32,0},{48,16},{64,96},{80,112},{96,64},{112,80},{1... | collective-permute-start | bytes 2064392 | tf_op jit(solution)/shard_map/ppermute | solution.py:24
  364.3 17.8 %collective-permute-start.2 = (bf16[448,768]{1,0:T(8,128)(2,1)S(1)}, bf16[448,768]{1,0:T(8,128)(2,1)}, u32[]{:S(2)}, u32[]{:S(2)}) collective-permute-start(bf16[448,768]{1,0:T(8,128)(2,1)S(1)} %collective-permute-done.1), channel_id=1, source_target_pairs={{0,64},{16,80},{32,96},{48,112},{64,0},{80,16},{96,32},{112,48},{1... | collective-permute-start | bytes 2064392 | tf_op jit(solution)/shard_map/ppermute | solution.py:24
  366.0 44.1 %collective-permute-start.11 = (bf16[192,3072]{1,0:T(8,128)(2,1)}, bf16[192,3072]{1,0:T(8,128)(2,1)}, u32[]{:S(2)}, u32[]{:S(2)}) collective-permute-start(bf16[192,3072]{1,0:T(8,128)(2,1)} %collective-permute-done.10), channel_id=1, source_target_pairs={{0,128},{16,144},{32,160},{48,176},{64,192},{80,208},{96,224},{112... | collective-permute-start | bytes 3538952 | tf_op jit(solution)/shard_map/ppermute | solution.py:24
  382.0 26.0 %collective-permute-start.3 = (bf16[448,768]{1,0:T(8,128)(2,1)}, bf16[448,768]{1,0:T(8,128)(2,1)S(1)}, u32[]{:S(2)}, u32[]{:S(2)}) collective-permute-start(bf16[448,768]{1,0:T(8,128)(2,1)} %collective-permute-done.2), channel_id=1, source_target_pairs={{0,128},{16,144},{32,160},{48,176},{64,192},{80,208},{96,224},{112... | collective-permute-start | bytes 2064392 | tf_op jit(solution)/shard_map/ppermute | solution.py:24
  391.1 19.0 %copy-start.10 = (bf16[192,3072]{1,0:T(8,128)(2,1)S(1)}, bf16[192,3072]{1,0:T(8,128)(2,1)}, u32[]{:S(2)}) copy-start(bf16[192,3072]{1,0:T(8,128)(2,1)} %reduce-scatter.5.cloned.1.call-done) | copy-start | bytes 3538948
  391.2 4.8 %collective-permute-start.4 = (bf16[192]{0:T(256)(128)(2,1)S(1)}, bf16[192]{0:T(256)(128)(2,1)S(1)}, u32[]{:S(2)}, u32[]{:S(2)}) collective-permute-start(bf16[192]{0:T(256)(128)(2,1)S(1)} %dynamic-slice.1), channel_id=1, source_target_pairs={{0,16},{16,0},{32,48},{48,32},{64,80},{80,64},{96,112},{112,96},{1... | collective-permute-start | bytes 1160 | tf_op jit(solution)/shard_map/ppermute | solution.py:24
  396.0 2.7 collective-permute-start.5
  398.7 3.9 collective-permute-start.6
  402.6 4.8 %collective-permute-start.7 = (bf16[192]{0:T(256)(128)(2,1)S(1)}, bf16[192]{0:T(256)(128)(2,1)S(1)}, u32[]{:S(2)}, u32[]{:S(2)}) collective-permute-start(bf16[192]{0:T(256)(128)(2,1)S(1)} %collective-permute-done.6), channel_id=1, source_target_pairs={{0,128},{16,144},{32,160},{48,176},{64,192},{80,208},{96,224},{112... | collective-permute-start | bytes 1160 | tf_op jit(solution)/shard_map/ppermute | solution.py:24
  (7 other events, 16.6 us)
Sparse Core Ops, SparseCore 0:
  9.9 53.9 all-gather.2
  65.7 50.6 all-gather.4
  157.9 61.6 all-reduce.3
  227.4 52.3 reduce-scatter.4
  282.2 37.3 reduce-scatter.2
where the time goes:
time: 421 us; the launch traced here: 419 us
  waiting for transfers between devices  275 us (65%)
  other arithmetic  82.5 us (20%)
  matrix products  22.6 us (5%)
  starting transfers between devices  17.3 us (4%)
  between operations  14.6 us (3%)
  blocking collectives  6.57 us (2%)
    select_n x32, other arithmetic, lap(): return jnp.where(reached, new, before)  74.9 us
    ppermute x12, waiting for transfers between devices, partner(): lax.ppermute(x, axis, [(i, i ^ 1 << distance) for i in range(lax.axis_siz...  67.5 us
    all_gather x2, waiting for transfers between devices, prefix(): everything = lax.all_gather(x.astype(jnp.bfloat16), axis)  62.8 us
    psum x1, waiting for transfers between devices, local(): lax.psum(jnp.einsum('th,qh->tq', query_grad_a, up_local, preferred_elemen...  61.7 us
    reduce_scatter x1, waiting for transfers between devices, local(): lax.psum_scatter(grad_up.astype(jnp.bfloat16), 'dp', scatter_dimension=0,...  45.9 us
    reduce_scatter x1, waiting for transfers between devices, local(): lax.psum_scatter(grad_downw.astype(jnp.bfloat16), 'dp', scatter_dimension...  35.2 us
    ppermute x12, starting transfers between devices, partner(): lax.ppermute(x, axis, [(i, i ^ 1 << distance) for i in range(lax.axis_siz...  17.1 us
  transfers between devices with their start and end apart: 17, of which 12 were waited for; matrix products, arithmetic and copies ran while one was open for 13% of the time, Pallas kernels for 0%

commit v1 on v0

v1 whole, which is shorter than its diff:
```python
import functools

import jax
import jax.numpy as jnp
from jax import lax
from jax.experimental import pallas as pl
from jax.experimental.pallas import tpu as pltpu
from jax.sharding import PartitionSpec as P

EPSILON = 1e-06
MESH = pl.DeviceIdType.MESH
F32 = jnp.float32
BF16 = jnp.bfloat16

TOK = 128
DM = 1792
QL = 768
HQ = 3072
CH = 8
BLK = TOK // CH
SUB = TOK // 4
DSH = DM // 4
USH = QL // 4
UCH = 4
UW = HQ // UCH
DCH = 2
DW = QL // DCH


def rows(i, n):
    return pl.ds(pl.multiple_of(i * n, n), n)


def kernel(
    attn_a, attn_b, w_down, gain, w_up, dq_a, dq_b,
    out_down, out_gain, out_up,
    att, xin, tot, got, pout, pfx, hid, dq, wd, wu,
    gnp, gnr, latp, latr, nz, gz, ntl, nall, gl, htl, hall,
    ubuf, urec, dbuf, drec, gbuf, grec,
    lsem, ss, rs,
):
    s, t, d = lax.axis_index("section"), lax.axis_index("tensor"), lax.axis_index("dp")
    chip, core = s // 2, s % 2

    def at_chip(j):
        return (j * 2 + core, t, d)

    def at_tensor(j):
        return (s, j, d)

    def at_dp(j):
        return (s, t, j)

    other_core = (chip * 2 + 1 - core, t, d)
    mirror = (15 - s, t, d)
    chips = [((chip + k) % CH) for k in range(1, CH)]
    tens = [((t + k) % 4) for k in range(1, 4)]
    dps = [((d + k) % 4) for k in range(1, 4)]

    counter = [0]
    sent = []

    def send(src, dst, to):
        i = counter[0]
        counter[0] += 1
        copy = pltpu.make_async_remote_copy(
            src_ref=src, dst_ref=dst, send_sem=ss.at[i], recv_sem=rs.at[i],
            device_id=to, device_id_type=MESH,
        )
        copy.start()
        sent.append(copy)
        return copy

    loads = []
    for i, (src, dst) in enumerate((
        (attn_a, att.at[0]),
        (attn_b, att.at[1]),
        (dq_a, dq.at[d, pl.ds(0, TOK)]),
        (dq_b, dq.at[d, pl.ds(TOK, TOK)]),
        (w_up, wu),
        (w_down, wd),
    )):
        c = pltpu.make_async_copy(src, dst, lsem.at[i])
        c.start()
        loads.append(c)

    barrier = pltpu.get_barrier_semaphore()
    partners = (
        [other_core, mirror]
        + [at_chip(j) for j in chips]
        + [at_tensor(j) for j in tens]
        + [at_dp(j) for j in dps]
    )
    for p in partners:
        pl.semaphore_signal(barrier, inc=1, device_id=p, device_id_type=MESH)
    pl.semaphore_wait(barrier, len(partners))

    loads[0].wait()
    loads[1].wait()
    swap = send(att.at[1 - core], xin, other_core)

    up, dn = (d + 1) % 4, (d + 3) % 4
    dq_up_a = send(dq_a, dq.at[d, pl.ds(0, TOK)], at_dp(up))
    dq_dn_b = send(dq_b, dq.at[d, pl.ds(TOK, TOK)], at_dp(dn))
    dq_up_b = send(dq_b, dq.at[d, pl.ds(TOK, TOK)], at_dp(up))
    dq_dn_a = send(dq_a, dq.at[d, pl.ds(0, TOK)], at_dp(dn))

    swap.wait_recv()
    tot[...] = (att[core].astype(F32) + xin[...].astype(F32)).astype(BF16)
    ph1 = [send(tot.at[rows(j, BLK)], got.at[chip], at_chip(j)) for j in chips]
    got[chip] = tot[rows(chip, BLK)]

    loads[2].wait()
    loads[3].wait()
    loads[4].wait()
    for m in range(2):
        gnp[m] = lax.dot_general(
            dq[d, m * TOK:(m + 1) * TOK], wu[...], (((1,), (1,)), ((), ())),
            preferred_element_type=F32,
        ).astype(BF16)
    gn = [send(gnp.at[:, rows(j, SUB)], gnr.at[k], at_tensor(j)) for k, j in enumerate(tens)]

    for c in ph1:
        c.wait_recv()
    run = jnp.zeros((BLK, DM), F32)
    for i in range(CH):
        j = i + core * (CH - 1 - 2 * i)
        pout[j] = run.astype(BF16)
        if i < CH - 1:
            run = run + got[j].astype(F32)
    ph2 = [send(pout.at[j], pfx.at[rows(chip, BLK)], at_chip(j)) for j in chips]
    pfx[rows(chip, BLK)] = pout[chip]
    for c in ph2:
        c.wait_recv()
    mine = pfx[...].astype(F32) + att[core].astype(F32)
    tot2 = xin
    tot2[...] = (mine + xin[...].astype(F32)).astype(BF16)
    back = send(tot2, hid.at[core], other_core)
    hid[core] = mine.astype(BF16)
    loads[5].wait()
    back.wait_recv()
    for m in range(2):
        latp[m] = jnp.dot(hid[m], wd[...], preferred_element_type=F32).astype(BF16)
    lt = [send(latp.at[:, rows(j, SUB)], latr.at[k], at_tensor(j)) for k, j in enumerate(tens)]

    for m in range(2):
        for q in range(4):
            for e in range(0, DSH, 64):
                lo = q * DSH + e
                base = lo // 128 * 128
                if lo % 128 == 0 and e + 128 <= DSH:
                    htl[q, e:e + 128, m * TOK:(m + 1) * TOK] = hid[m, :, lo:lo + 128].T
                elif lo % 128 == 0:
                    htl[q, e:e + 64, m * TOK:(m + 1) * TOK] = hid[m, :, base:base + 128].T[0:64]
                elif e == 0:
                    htl[q, 0:64, m * TOK:(m + 1) * TOK] = hid[m, :, base:base + 128].T[64:128]
    ht = [send(htl.at[j], hall.at[d], at_dp(j)) for j in dps]
    hall[d] = htl[d]

    for c in gn + lt:
        c.wait_recv()

    def total(part, recv):
        x = part[:, rows(t, SUB)].astype(F32)
        for k in range(3):
            x = x + recv[k].astype(F32)
        return x.reshape(2 * SUB, QL)

    lat = total(latp, latr)
    gnrm = total(gnp, gnr)
    g = gain[...].astype(F32)
    inv = lax.rsqrt(jnp.mean(lat * lat, axis=-1, keepdims=True) + EPSILON)
    nz[t] = (lat * inv * g).astype(BF16)
    an = [send(nz.at[t], nz.at[t], at_tensor(j)) for j in tens]
    scaled = gnrm * g
    glat = inv * scaled - lat * (inv * inv * inv) * jnp.mean(scaled * lat, axis=-1, keepdims=True)

    def hi_lo(v):
        hi = v.astype(BF16)
        lo = (v - hi.astype(F32)).astype(BF16)
        r = lax.broadcasted_iota(jnp.int32, (16, QL), 0)
        return jnp.where(r == 0, hi.astype(F32), jnp.where(r == 1, lo.astype(F32), 0.0)).astype(BF16)

    gz[t, 0:2 * SUB] = glat.astype(BF16)
    gz[t, 2 * SUB:2 * SUB + 16] = hi_lo(jnp.sum(gnrm * lat * inv, axis=0, keepdims=True))
    ag = [send(gz.at[t], gz.at[t], at_tensor(j)) for j in tens]

    dq_up_a.wait_recv()
    fw_up = send(dq.at[dn, pl.ds(0, TOK)], dq.at[dn, pl.ds(0, TOK)], at_dp(up))
    dq_dn_b.wait_recv()
    fw_dn = send(dq.at[up, pl.ds(TOK, TOK)], dq.at[up, pl.ds(TOK, TOK)], at_dp(dn))

    for c in an:
        c.wait_recv()
    for m in range(2):
        full = jnp.concatenate([nz[k, m * SUB:(m + 1) * SUB] for k in range(4)], axis=0)
        for q in range(QL // 64):
            if q % 2 == 0:
                tr = full[:, q * 64:q * 64 + 128].T
            dst, off = q * 64 // USH, q * 64 % USH
            ntl[dst, off:off + 64, m * TOK:(m + 1) * TOK] = tr[(q % 2) * 64:(q % 2) * 64 + 64]
    nt = [send(ntl.at[j], nall.at[d], at_dp(j)) for j in dps]
    nall[d] = ntl[d]

    for c in ag:
        c.wait_recv()
    for m in range(2):
        for k in range(4):
            gl[d, m * TOK + k * SUB:m * TOK + (k + 1) * SUB] = gz[k, m * SUB:(m + 1) * SUB]

    def gain_rows(parts):
        v = jnp.zeros((1, QL), F32)
        for x in parts:
            v = v + jnp.sum(x.astype(F32), axis=0, keepdims=True)
        return v

    gl[d, 2 * TOK:2 * TOK + 16] = hi_lo(gain_rows([gz[k, 2 * SUB:2 * SUB + 16] for k in range(4)]))
    ga = [send(gl.at[d], gl.at[d], at_dp(j)) for j in dps]

    for c in nt:
        c.wait_recv()
    for c in (dq_up_b, dq_dn_a, fw_up, fw_dn):
        c.wait_recv()
    ups = []
    for n in range(UCH):
        acc = jnp.zeros((USH, UW), F32)
        for k in range(4):
            acc = acc + jnp.dot(
                nall[k], dq[k, :, n * UW:(n + 1) * UW], preferred_element_type=F32
            )
        ubuf[n] = acc.astype(BF16)
        ups.append(send(ubuf.at[n], urec.at[n], mirror))

    for c in ga + ht:
        c.wait_recv()
    gbuf[...] = jnp.broadcast_to(
        gain_rows([gl[k, 2 * TOK:2 * TOK + 16] for k in range(4)]), (16, QL)
    ).astype(BF16)
    gsend = send(gbuf, grec, mirror)
    downs = []
    for n in range(DCH):
        acc = jnp.zeros((DSH, DW), F32)
        for k in range(4):
            acc = acc + jnp.dot(
                hall[k], gl[k, 0:2 * TOK, n * DW:(n + 1) * DW], preferred_element_type=F32
            )
        dbuf[n] = acc.astype(BF16)
        downs.append(send(dbuf.at[n], drec.at[n], mirror))

    gsend.wait_recv()
    both = (gbuf[0:1].astype(F32) + grec[0:1].astype(F32))
    pick = both[:, 0:USH]
    for q in range(1, 4):
        pick = jnp.where(d == q, both[:, q * USH:(q + 1) * USH], pick)
    out_gain[...] = pick.astype(BF16)
    for n in range(UCH):
        ups[n].wait_recv()
        out_up[:, n * UW:(n + 1) * UW] = (ubuf[n].astype(F32) + urec[n].astype(F32)).astype(BF16)
    for n in range(DCH):
        downs[n].wait_recv()
        out_down[:, n * DW:(n + 1) * DW] = (dbuf[n].astype(F32) + drec[n].astype(F32)).astype(BF16)
    for c in sent:
        c.wait_send()


NCOPY = 1 + 4 + 7 + 3 + 7 + 1 + 3 + 3 + 3 + 3 + 2 + 3 + 3 + UCH + 1 + DCH


def local(attn_a, attn_b, w_down, q_gain, w_up, dq_a, dq_b):
    anywhere = pl.BlockSpec(memory_space=pl.ANY)
    vmem = pl.BlockSpec(memory_space=pltpu.VMEM)
    shapes = [
        (2, TOK, DM), (TOK, DM), (TOK, DM), (CH, BLK, DM), (CH, BLK, DM), (TOK, DM), (2, TOK, DM),
        (4, 2 * TOK, HQ), (DM, QL), (QL, HQ),
        (2, TOK, QL), (3, 2, SUB, QL), (2, TOK, QL), (3, 2, SUB, QL),
        (4, 2 * SUB, QL), (4, 2 * SUB + 16, QL),
        (4, USH, 2 * TOK), (4, USH, 2 * TOK), (4, 2 * TOK + 16, QL),
        (4, DSH, 2 * TOK), (4, DSH, 2 * TOK),
        (UCH, USH, UW), (UCH, USH, UW), (DCH, DSH, DW), (DCH, DSH, DW), (16, QL), (16, QL),
    ]
    down, gain, up = pl.pallas_call(
        kernel,
        out_shape=(
            jax.ShapeDtypeStruct((DSH, QL), BF16),
            jax.ShapeDtypeStruct((1, USH), BF16),
            jax.ShapeDtypeStruct((USH, HQ), BF16),
        ),
        in_specs=[anywhere, anywhere, anywhere, vmem, anywhere, anywhere, anywhere],
        out_specs=(vmem, vmem, vmem),
        scratch_shapes=[pltpu.VMEM(x, BF16) for x in shapes] + [
            pltpu.SemaphoreType.DMA((6,)),
            pltpu.SemaphoreType.DMA((NCOPY,)),
            pltpu.SemaphoreType.DMA((NCOPY,)),
        ],
        compiler_params=pltpu.CompilerParams(
            collective_id=0, has_side_effects=True, vmem_limit_bytes=56 * 2**20
        ),
        name="sections",
    )(attn_a[0], attn_b[0], w_down[0], q_gain, w_up[0], dq_a[0], dq_b[0])
    return down[None], gain, up[None]


def solution(mesh):
    return jax.shard_map(
        local,
        mesh=mesh,
        in_specs=(
            P("section", "dp", "tensor"),
            P("section", "dp", "tensor"),
            P("section", "tensor", None),
            P("section", None),
            P("section", None, "tensor"),
            P("section", "dp", "tensor"),
            P("section", "dp", "tensor"),
        ),
        out_specs=(
            P("section", ("tensor", "dp"), None),
            P("section", "dp"),
            P("section", "dp", "tensor"),
        ),
        check_vma=False,
    )
```

time: 421 us -> 130 us (0.31)
  waiting for transfers between devices: 275 us -> 0 us
  Pallas kernels: 0 us -> 124 us
  other arithmetic: 82.5 us -> 0 us
  matrix products: 22.6 us -> 0 us
  starting transfers between devices: 17.3 us -> 0 us
  between operations: 14.6 us -> 0.64 us
  blocking collectives: 6.57 us -> 0 us
  local copies, waits for them, and re-layouts: 1.3 us -> 5.57 us
    pallas_call x0 -> x1, Pallas kernels: none -> 124 us  [local(): pl.pallas_call(kernel, out_shape=(jax.ShapeDtypeStruct((DSH, QL), BF16),...]
    reduce_scatter x2 -> x0, waiting for transfers between devices: 81.1 us -> none  [the longest x1 45.9 us: local(): lax.psum_scatter(grad_up.astype(jnp.bfloat16), 'dp', scatter_dimension=0,...]
    select_n x32 -> x0, other arithmetic: 74.9 us -> none  [lap(): return jnp.where(reached, new, before)]
    ppermute x12 -> x0, waiting for transfers between devices: 67.5 us -> none  [partner(): lax.ppermute(x, axis, [(i, i ^ 1 << distance) for i in range(lax.axis_siz...]
    all_gather x2 -> x0, waiting for transfers between devices: 62.8 us -> none  [prefix(): everything = lax.all_gather(x.astype(jnp.bfloat16), axis)]
    psum x1 -> x0, waiting for transfers between devices: 61.7 us -> none  [local(): lax.psum(jnp.einsum('th,qh->tq', query_grad_a, up_local, preferred_elemen...]
    dot_general x8 -> x0, matrix products: 22.6 us -> none  [the longest x1 5.08 us: local(): jnp.einsum('th,qh->tq', query_grad_a, up_local, preferred_element_type=jn...]
    ppermute x12 -> x0, starting transfers between devices: 17.1 us -> none  [partner(): lax.ppermute(x, axis, [(i, i ^ 1 << distance) for i in range(lax.axis_siz...]
  transfers between devices with their start and end apart: 17 -> 0, of which waited for: 12 -> 0; matrix products, arithmetic and copies ran while one was open for 13% -> 0% of each run, Pallas kernels for 0% -> 0%
where the time goes in v1:
time: 130 us
  Pallas kernels  124 us (95%)
  local copies, waits for them, and re-layouts  5.57 us (4%)
    pallas_call x1, Pallas kernels, local(): pl.pallas_call(kernel, out_shape=(jax.ShapeDtypeStruct((DSH, QL), BF16),...  124 us
    unnamed x3, local copies, waits for them, and re-layouts  5.57 us

profile of v1, /device:TPU:1, one launch (start us, length us, event | category | flops | bytes accessed | tf_op | source)
XLA Modules:
  0.0 129.7 jit_solution(10334449182683796276)
XLA Ops:
  0.6 123.5 %sections.1 = (bf16[448,768]{1,0:T(8,128)(2,1)}, bf16[1,192]{1,0:T(2,128)(2,1)}, bf16[192,3072]{1,0:T(8,128)(2,1)}) custom-call(bf16[128,1792]{1,0:T(8,128)(2,1)} %bitcast.14, bf16[128,1792]{1,0:T(8,128)(2,1)} %bitcast.15, bf16[1792,768]{1,0:T(8,128)(2,1)} %bitcast.9, bf16[1,768]{1,0:T(2,128)(2,1)} %gain.1, bf16[768,3072]{1,0:T(8,128)(2,1)} %bitcast.8, ...), custom_call_target="tpu_custom_call" | custom-call | tf_op jit(solution)/shard_map/sections/pallas_call | solution.py:281
  124.2 2.0 %copy.13 = bf16[1,448,768]{2,1,0:T(8,128)(2,1)} copy(bf16[1,448,768]{2,1,0:T(8,128)(2,1)} %bitcast.13) | data formatting | bytes 1376256
  126.2 1.2 copy.14
  127.4 2.4 %copy.15 = bf16[1,192,3072]{2,1,0:T(8,128)(2,1)} copy(bf16[1,192,3072]{2,1,0:T(8,128)(2,1)} %bitcast.10) | data formatting | bytes 2359296

commit v2 on v1

v2 whole, which is shorter than its diff:
```python
import functools

import jax
import jax.numpy as jnp
from jax import lax
from jax.experimental import pallas as pl
from jax.experimental.pallas import tpu as pltpu
from jax.sharding import PartitionSpec as P

EPSILON = 1e-06
MESH = pl.DeviceIdType.MESH
F32 = jnp.float32
BF16 = jnp.bfloat16

TOK = 128
DM = 1792
QL = 768
HQ = 3072
CH = 8
BLK = TOK // CH
SUB = TOK // 4
DSH = DM // 4
USH = QL // 4
UCH = 4
UW = HQ // UCH
DCH = 2
DW = QL // DCH
HW = HQ // 2
NCOPY = 96


def rows(i, n):
    return pl.ds(pl.multiple_of(i * n, n), n)


def kernel(
    attn_a, attn_b, w_down, gain, w_up, dq_a, dq_b,
    u_own, u_rec, d_own, d_rec, g_own, g_rec,
    att, xin, tot, got, pout, pfx, hid, dq, wd, wu,
    gnp, gnr, latp, latr, nz, gz, ntl, nall, gl, gg, htl, hall,
    ubuf, dbuf, gbuf,
    lsem, ss, rs,
):
    s, t, d = lax.axis_index("section"), lax.axis_index("tensor"), lax.axis_index("dp")
    chip, core = s // 2, s % 2

    def at_chip(j):
        return (j * 2 + core, t, d)

    def at_tensor(j):
        return (s, j, d)

    def at_dp(j):
        return (s, t, j)

    other_core = (chip * 2 + 1 - core, t, d)
    mirror = (15 - s, t, d)
    chips = [((chip + k) % CH) for k in range(1, CH)]
    tens = [((t + k) % 4) for k in range(1, 4)]
    dps = [((d + k) % 4) for k in range(1, 4)]
    up, dn = (d + 1) % 4, (d + 3) % 4
    lo, hi = pl.ds(0, TOK), pl.ds(TOK, TOK)

    counter = [0]
    sent = []

    def send(src, dst, to):
        i = counter[0]
        counter[0] += 1
        copy = pltpu.make_async_remote_copy(
            src_ref=src, dst_ref=dst, send_sem=ss.at[i], recv_sem=rs.at[i],
            device_id=to, device_id_type=MESH,
        )
        copy.start()
        sent.append(copy)
        return copy

    loads = []

    def load(src, dst):
        c = pltpu.make_async_copy(src, dst, lsem.at[len(loads)])
        c.start()
        loads.append(c)
        return c

    ld_a = load(attn_a, att.at[0])
    ld_b = load(attn_b, att.at[1])

    barrier = pltpu.get_barrier_semaphore()
    partners = (
        [other_core, mirror]
        + [at_chip(j) for j in chips]
        + [at_tensor(j) for j in tens]
        + [at_dp(j) for j in dps]
    )
    for p in partners:
        pl.semaphore_signal(barrier, inc=1, device_id=p, device_id_type=MESH)
    pl.semaphore_wait(barrier, len(partners))

    ld_a.wait()
    ld_b.wait()
    swap = send(att.at[1 - core], xin, other_core)

    def dq_out(h):
        c = pl.ds(h * HW, HW)
        return (
            send(dq_a.at[:, c], dq.at[d, lo, c], at_dp(up)),
            send(dq_b.at[:, c], dq.at[d, hi, c], at_dp(dn)),
            send(dq_b.at[:, c], dq.at[d, hi, c], at_dp(up)),
            send(dq_a.at[:, c], dq.at[d, lo, c], at_dp(dn)),
        )

    def dq_forward(h, out):
        c = pl.ds(h * HW, HW)
        out[0].wait_recv()
        f = send(dq.at[dn, lo, c], dq.at[dn, lo, c], at_dp(up))
        out[1].wait_recv()
        return f, send(dq.at[up, hi, c], dq.at[up, hi, c], at_dp(dn))

    out0 = dq_out(0)
    ld_up = load(w_up, wu)
    ld_qa = load(dq_a, dq.at[d, lo])
    ld_qb = load(dq_b, dq.at[d, hi])
    ld_down = load(w_down, wd)

    swap.wait_recv()
    tot[...] = (att[core].astype(F32) + xin[...].astype(F32)).astype(BF16)
    ph1 = [send(tot.at[rows(j, BLK)], got.at[chip], at_chip(j)) for j in chips]
    got[chip] = tot[rows(chip, BLK)]

    ld_qa.wait()
    ld_qb.wait()
    ld_up.wait()
    for m in range(2):
        gnp[m] = lax.dot_general(
            dq[d, m * TOK:(m + 1) * TOK], wu[...], (((1,), (1,)), ((), ())),
            preferred_element_type=F32,
        ).astype(BF16)

    for c in ph1:
        c.wait_recv()
    run = jnp.zeros((BLK, DM), F32)
    for i in range(CH):
        j = i + core * (CH - 1 - 2 * i)
        pout[j] = run.astype(BF16)
        if i < CH - 1:
            run = run + got[j].astype(F32)
    ph2 = [send(pout.at[j], pfx.at[rows(chip, BLK)], at_chip(j)) for j in chips]
    pfx[rows(chip, BLK)] = pout[chip]
    gn = [send(gnp.at[:, rows(j, SUB)], gnr.at[k], at_tensor(j)) for k, j in enumerate(tens)]
    out1 = dq_out(1)

    for c in ph2:
        c.wait_recv()
    mine = pfx[...].astype(F32) + att[core].astype(F32)
    tot2 = xin
    tot2[...] = (mine + xin[...].astype(F32)).astype(BF16)
    back = send(tot2, hid.at[core], other_core)
    hid[core] = mine.astype(BF16)

    ld_down.wait()
    lt = []
    for m in (core, 1 - core):
        if lt:
            back.wait_recv()
        latp[m] = jnp.dot(hid[m], wd[...], preferred_element_type=F32).astype(BF16)
        lt += [
            send(latp.at[m, rows(j, SUB)], latr.at[k, m], at_tensor(j)) for k, j in enumerate(tens)
        ]

    for m in range(2):
        for q in range(4):
            for e in range(0, DSH, 64):
                at = q * DSH + e
                base = at // 128 * 128
                if at % 128 == 0 and e + 128 <= DSH:
                    htl[q, e:e + 128, m * TOK:(m + 1) * TOK] = hid[m, :, at:at + 128].T
                elif at % 128 == 0:
                    htl[q, e:e + 64, m * TOK:(m + 1) * TOK] = hid[m, :, base:base + 128].T[0:64]
                elif e == 0:
                    htl[q, 0:64, m * TOK:(m + 1) * TOK] = hid[m, :, base:base + 128].T[64:128]
    hall[d] = htl[d]
    fw0 = dq_forward(0, out0)

    for c in lt:
        c.wait_recv()

    def total(part, recv):
        x = part[:, rows(t, SUB)].astype(F32)
        for k in range(3):
            x = x + recv[k].astype(F32)
        return x.reshape(2 * SUB, QL)

    lat = total(latp, latr)
    g = gain[...].astype(F32)
    inv = lax.rsqrt(jnp.mean(lat * lat, axis=-1, keepdims=True) + EPSILON)
    nz[t] = (lat * inv * g).astype(BF16)
    an = [send(nz.at[t], nz.at[t], at_tensor(j)) for j in tens]

    def hi_lo(v):
        high = v.astype(BF16)
        low = (v - high.astype(F32)).astype(BF16)
        r = lax.broadcasted_iota(jnp.int32, (16, QL), 0)
        both = jnp.where(r == 0, high.astype(F32), jnp.where(r == 1, low.astype(F32), 0.0))
        return both.astype(BF16)

    for c in gn:
        c.wait_recv()
    gnrm = total(gnp, gnr)
    scaled = gnrm * g
    glat = inv * scaled - lat * (inv * inv * inv) * jnp.mean(scaled * lat, axis=-1, keepdims=True)
    gz[t, 0:2 * SUB] = glat.astype(BF16)
    gz[t, 2 * SUB:2 * SUB + 16] = hi_lo(jnp.sum(gnrm * lat * inv, axis=0, keepdims=True))

    fw1 = dq_forward(1, out1)

    for c in an:
        c.wait_recv()
    ag = [send(gz.at[t], gz.at[t], at_tensor(j)) for j in tens]
    for m in range(2):
        full = jnp.concatenate([nz[k, m * SUB:(m + 1) * SUB] for k in range(4)], axis=0)
        for q in range(QL // 64):
            if q % 2 == 0:
                tr = full[:, q * 64:q * 64 + 128].T
            dst, off = q * 64 // USH, q * 64 % USH
            ntl[dst, off:off + 64, m * TOK:(m + 1) * TOK] = tr[(q % 2) * 64:(q % 2) * 64 + 64]
    nt = [send(ntl.at[j], nall.at[d], at_dp(j)) for j in dps]
    nall[d] = ntl[d]
    ht = [send(htl.at[j], hall.at[d], at_dp(j)) for j in dps]

    for c in nt:
        c.wait_recv()
    ups = []
    for n in range(UCH):
        if n % (UCH // 2) == 0:
            h = n // (UCH // 2)
            for c in ((out0, out1)[h][2], (out0, out1)[h][3]) + (fw0, fw1)[h]:
                c.wait_recv()
        acc = jnp.zeros((USH, UW), F32)
        for k in range(4):
            acc = acc + jnp.dot(
                nall[k], dq[k, :, n * UW:(n + 1) * UW], preferred_element_type=F32
            )
        ubuf[n] = acc.astype(BF16)
        ups.append(send(ubuf.at[n], u_rec.at[n], mirror))
        load(ubuf.at[n], u_own.at[n])

    for c in ag:
        c.wait_recv()
    for n in range(DCH):
        for m in range(2):
            for k in range(4):
                gl[n, d, m * TOK + k * SUB:m * TOK + (k + 1) * SUB] = gz[
                    k, m * SUB:(m + 1) * SUB, n * DW:(n + 1) * DW
                ]

    def gain_rows(parts):
        v = jnp.zeros((1, QL), F32)
        for x in parts:
            v = v + jnp.sum(x.astype(F32), axis=0, keepdims=True)
        return v

    gg[d] = hi_lo(gain_rows([gz[k, 2 * SUB:2 * SUB + 16] for k in range(4)]))
    gs = [send(gg.at[d], gg.at[d], at_dp(j)) for j in dps]
    ga = [[send(gl.at[n, d], gl.at[n, d], at_dp(j)) for j in dps] for n in range(DCH)]

    for c in gs:
        c.wait_recv()
    sums = gain_rows([gg[k] for k in range(4)])
    pick = sums[:, 0:USH]
    for q in range(1, 4):
        pick = jnp.where(d == q, sums[:, q * USH:(q + 1) * USH], pick)
    gbuf[...] = jnp.broadcast_to(pick, (16, USH)).astype(BF16)
    last = [send(gbuf, g_rec, mirror)]
    load(gbuf, g_own)

    for c in ht:
        c.wait_recv()
    for n in range(DCH):
        for c in ga[n]:
            c.wait_recv()
        acc = jnp.zeros((DSH, DW), F32)
        for k in range(4):
            acc = acc + jnp.dot(hall[k], gl[n, k], preferred_element_type=F32)
        dbuf[n] = acc.astype(BF16)
        last.append(send(dbuf.at[n], d_rec.at[n], mirror))
        load(dbuf.at[n], d_own.at[n])

    for c in ups + last:
        c.wait_recv()
    for c in loads[6:]:
        c.wait()
    for c in sent:
        c.wait_send()


def finish(u_own, u_rec, d_own, d_rec, g_own, g_rec, down, gain, up):
    up[...] = (u_own[0].astype(F32) + u_rec[0].astype(F32)).astype(BF16)
    down[...] = (d_own[0].astype(F32) + d_rec[0].astype(F32)).astype(BF16)
    gain[...] = (g_own[0:1].astype(F32) + g_rec[0:1].astype(F32)).astype(BF16)


def local(attn_a, attn_b, w_down, q_gain, w_up, dq_a, dq_b):
    anywhere = pl.BlockSpec(memory_space=pl.ANY)
    vmem = pl.BlockSpec(memory_space=pltpu.VMEM)
    shapes = [
        (2, TOK, DM), (TOK, DM), (TOK, DM), (CH, BLK, DM), (CH, BLK, DM), (TOK, DM), (2, TOK, DM),
        (4, 2 * TOK, HQ), (DM, QL), (QL, HQ),
        (2, TOK, QL), (3, 2, SUB, QL), (2, TOK, QL), (3, 2, SUB, QL),
        (4, 2 * SUB, QL), (4, 2 * SUB + 16, QL),
        (4, USH, 2 * TOK), (4, USH, 2 * TOK), (DCH, 4, 2 * TOK, DW), (4, 16, QL),
        (4, DSH, 2 * TOK), (4, DSH, 2 * TOK),
        (UCH, USH, UW), (DCH, DSH, DW), (16, USH),
    ]
    halves = [(UCH, USH, UW)] * 2 + [(DCH, DSH, DW)] * 2 + [(16, USH)] * 2
    parts = pl.pallas_call(
        kernel,
        out_shape=[jax.ShapeDtypeStruct(x, BF16) for x in halves],
        in_specs=[anywhere, anywhere, anywhere, vmem, anywhere, anywhere, anywhere],
        out_specs=[anywhere] * 6,
        scratch_shapes=[pltpu.VMEM(x, BF16) for x in shapes] + [
            pltpu.SemaphoreType.DMA((16,)),
            pltpu.SemaphoreType.DMA((NCOPY,)),
            pltpu.SemaphoreType.DMA((NCOPY,)),
        ],
        compiler_params=pltpu.CompilerParams(
            collective_id=0, has_side_effects=True, vmem_limit_bytes=56 * 2**20
        ),
        name="sections",
    )(attn_a[0], attn_b[0], w_down[0], q_gain, w_up[0], dq_a[0], dq_b[0])
    ublock = pl.BlockSpec((1, USH, UW), lambda n: (n, 0, 0))
    dblock = pl.BlockSpec((1, DSH // 2, DW), lambda n: (n // 2, n % 2, 0))
    gblock = pl.BlockSpec((16, USH), lambda n: (0, 0))
    down, gain, up = pl.pallas_call(
        finish,
        grid=(4,),
        out_shape=(
            jax.ShapeDtypeStruct((DSH, QL), BF16),
            jax.ShapeDtypeStruct((1, USH), BF16),
            jax.ShapeDtypeStruct((USH, HQ), BF16),
        ),
        in_specs=[ublock, ublock, dblock, dblock, gblock, gblock],
        out_specs=(
            pl.BlockSpec((DSH // 2, DW), lambda n: (n % 2, n // 2)),
            pl.BlockSpec((1, USH), lambda n: (0, 0)),
            pl.BlockSpec((USH, UW), lambda n: (0, n)),
        ),
        compiler_params=pltpu.CompilerParams(vmem_limit_bytes=56 * 2**20),
        name="finish",
    )(*parts)
    return down[None], gain, up[None]


def solution(mesh):
    return jax.shard_map(
        local,
        mesh=mesh,
        in_specs=(
            P("section", "dp", "tensor"),
            P("section", "dp", "tensor"),
            P("section", "tensor", None),
            P("section", None),
            P("section", None, "tensor"),
            P("section", "dp", "tensor"),
            P("section", "dp", "tensor"),
        ),
        out_specs=(
            P("section", ("tensor", "dp"), None),
            P("section", "dp"),
            P("section", "dp", "tensor"),
        ),
        check_vma=False,
    )
```

time: 130 us -> 118 us (0.908)
  Pallas kernels: 124 us -> 117 us
  local copies, waits for them, and re-layouts: 5.57 us -> 0 us
    pallas_call x1 -> x2, Pallas kernels: 124 us -> 117 us  [the longest x1 113 us: local(): pl.pallas_call(kernel, out_shape=[jax.ShapeDtypeStruct(x, BF16) for x in...]
    unnamed x3 -> x0, local copies, waits for them, and re-layouts: 5.57 us -> none
where the time goes in v2:
time: 118 us
  Pallas kernels  117 us (99%)
    pallas_call x1, Pallas kernels, local(): pl.pallas_call(kernel, out_shape=[jax.ShapeDtypeStruct(x, BF16) for x in...  113 us
    pallas_call x1, Pallas kernels, local(): pl.pallas_call(finish, grid=(4,), out_shape=(jax.ShapeDtypeStruct((DSH, Q...  4.07 us

profile of v2, /device:TPU:1, one launch (start us, length us, event | category | flops | bytes accessed | tf_op | source)
XLA Modules:
  0.0 117.7 jit_solution(279212818725376128)
XLA Ops:
  0.6 113.0 %sections.1 = (bf16[4,192,768]{2,1,0:T(8,128)(2,1)}, bf16[4,192,768]{2,1,0:T(8,128)(2,1)}, bf16[2,448,384]{2,1,0:T(8,128)(2,1)}, bf16[2,448,384]{2,1,0:T(8,128)(...) custom-call(bf16[128,1792]{1,0:T(8,128)(2,1)} %bitcast.12, bf16[128,1792]{1,0:T(8,128)(2,1)} %bitcast.13, ...), custom_call_target="tpu_custom_call" | custom-call | tf_op jit(solution)/shard_map/sections/pallas_call | solution.py:316
  113.7 4.1 %finish.1 = (bf16[448,768]{1,0:T(8,128)(2,1)}, bf16[1,192]{1,0:T(2,128)(2,1)}, bf16[192,3072]{1,0:T(8,128)(2,1)}) custom-call(bf16[4,192,768]{2,1,0:T(8,128)(2,1)} %get-tuple-element.12.u_own, bf16[4,192,768]{2,1,0:T(8,128)(2,1)} %get-tuple-element.13.u_rec, bf16[2,448,384]{2,1,0:T(8,128)(2,1)} %get-tuple-element.14.d_own, ...), custom_call_target="tpu_custom_call" | custom-call | tf_op jit(solution)/shard_map/finish/pallas_call | solution.py:334

commit v3 on v2

--- a/solution.py
+++ b/solution.py
@@ -16,8 +16,7 @@
 DM = 1792
 QL = 768
 HQ = 3072
-CH = 8
-BLK = TOK // CH
+BLK = 16
 SUB = TOK // 4
 DSH = DM // 4
 USH = QL // 4
@@ -25,7 +24,6 @@
 UW = HQ // UCH
 DCH = 2
 DW = QL // DCH
-HW = HQ // 2
 NCOPY = 96
 
 
@@ -36,7 +34,7 @@
 def kernel(
     attn_a, attn_b, w_down, gain, w_up, dq_a, dq_b,
     u_own, u_rec, d_own, d_rec, g_own, g_rec,
-    att, xin, tot, got, pout, pfx, hid, dq, wd, wu,
+    att, xin, tot, got, pre, zout, zin, pout, pfx, hid, dq, wd, wu,
     gnp, gnr, latp, latr, nz, gz, ntl, nall, gl, gg, htl, hall,
     ubuf, dbuf, gbuf,
     lsem, ss, rs,
@@ -44,8 +42,10 @@
     s, t, d = lax.axis_index("section"), lax.axis_index("tensor"), lax.axis_index("dp")
     chip, core = s // 2, s % 2
 
-    def at_chip(j):
-        return (j * 2 + core, t, d)
+    zlo, x = chip // 4, chip % 4
+
+    def at_x(j):
+        return (zlo * 8 + j * 2 + core, t, d)
 
     def at_tensor(j):
         return (s, j, d)
@@ -55,7 +55,8 @@
 
     other_core = (chip * 2 + 1 - core, t, d)
     mirror = (15 - s, t, d)
-    chips = [((chip + k) % CH) for k in range(1, CH)]
+    other_row = ((s + 8) % 16, t, d)
+    xs = [((x + k) % 4) for k in range(1, 4)]
     tens = [((t + k) % 4) for k in range(1, 4)]
     dps = [((d + k) % 4) for k in range(1, 4)]
     up, dn = (d + 1) % 4, (d + 3) % 4
@@ -88,8 +89,8 @@
 
     barrier = pltpu.get_barrier_semaphore()
     partners = (
-        [other_core, mirror]
-        + [at_chip(j) for j in chips]
+        [other_core, mirror, other_row]
+        + [at_x(j) for j in xs]
         + [at_tensor(j) for j in tens]
         + [at_dp(j) for j in dps]
     )
@@ -97,12 +98,8 @@
         pl.semaphore_signal(barrier, inc=1, device_id=p, device_id_type=MESH)
     pl.semaphore_wait(barrier, len(partners))
 
-    ld_a.wait()
-    ld_b.wait()
-    swap = send(att.at[1 - core], xin, other_core)
-
     def dq_out(h):
-        c = pl.ds(h * HW, HW)
+        c = pl.ds(h * UW, UW)
         return (
             send(dq_a.at[:, c], dq.at[d, lo, c], at_dp(up)),
             send(dq_b.at[:, c], dq.at[d, hi, c], at_dp(dn)),
@@ -110,23 +107,28 @@
             send(dq_a.at[:, c], dq.at[d, lo, c], at_dp(dn)),
         )
 
-    def dq_forward(h, out):
-        c = pl.ds(h * HW, HW)
-        out[0].wait_recv()
+    def dq_forward(h):
+        c = pl.ds(h * UW, UW)
+        out[h][0].wait_recv()
         f = send(dq.at[dn, lo, c], dq.at[dn, lo, c], at_dp(up))
-        out[1].wait_recv()
+        out[h][1].wait_recv()
         return f, send(dq.at[up, hi, c], dq.at[up, hi, c], at_dp(dn))
 
-    out0 = dq_out(0)
-    ld_up = load(w_up, wu)
+    ld_a.wait()
+    ld_b.wait()
+    swap = send(att.at[1 - core], xin, other_core)
+    out = [dq_out(0), dq_out(1)]
     ld_qa = load(dq_a, dq.at[d, lo])
     ld_qb = load(dq_b, dq.at[d, hi])
+    ld_up = load(w_up, wu)
     ld_down = load(w_down, wd)
 
     swap.wait_recv()
     tot[...] = (att[core].astype(F32) + xin[...].astype(F32)).astype(BF16)
-    ph1 = [send(tot.at[rows(j, BLK)], got.at[chip], at_chip(j)) for j in chips]
-    got[chip] = tot[rows(chip, BLK)]
+    ph1 = []
+    for h in range(2):
+        ph1.append([send(tot.at[rows(j * 2 + h, BLK)], got.at[h, x], at_x(j)) for j in xs])
+        got[h, x] = tot[rows(x * 2 + h, BLK)]
 
     ld_qa.wait()
     ld_qb.wait()
@@ -137,18 +139,32 @@
             preferred_element_type=F32,
         ).astype(BF16)
 
-    for c in ph1:
-        c.wait_recv()
-    run = jnp.zeros((BLK, DM), F32)
-    for i in range(CH):
-        j = i + core * (CH - 1 - 2 * i)
-        pout[j] = run.astype(BF16)
-        if i < CH - 1:
-            run = run + got[j].astype(F32)
-    ph2 = [send(pout.at[j], pfx.at[rows(chip, BLK)], at_chip(j)) for j in chips]
-    pfx[rows(chip, BLK)] = pout[chip]
+    totals = []
+    for h in range(2):
+        for c in ph1[h]:
+            c.wait_recv()
+        run = jnp.zeros((BLK, DM), F32)
+        for i in range(4):
+            j = i + core * (3 - 2 * i)
+            pre[h, j] = run
+            run = run + got[h, j].astype(F32)
+        zout[h] = run.astype(BF16)
+        totals.append(send(zout.at[h], zin.at[h], other_row))
+
     gn = [send(gnp.at[:, rows(j, SUB)], gnr.at[k], at_tensor(j)) for k, j in enumerate(tens)]
-    out1 = dq_out(1)
+    out.append(dq_out(2))
+
+    ph2 = []
+    behind = zlo + core == 1
+    for h in range(2):
+        totals[h].wait_recv()
+        far = jnp.where(behind, zin[h].astype(F32), 0.0)
+        for j in range(4):
+            pout[h, j] = (pre[h, j] + far).astype(BF16)
+        ph2 += [send(pout.at[h, j], pfx.at[rows(x * 2 + h, BLK)], at_x(j)) for j in xs]
+        pfx[rows(x * 2 + h, BLK)] = pout[h, x]
+    out.append(dq_out(3))
+    fw = [dq_forward(0)]
 
     for c in ph2:
         c.wait_recv()
@@ -164,9 +180,10 @@
         if lt:
             back.wait_recv()
         latp[m] = jnp.dot(hid[m], wd[...], preferred_element_type=F32).astype(BF16)
-        lt += [
+        lt.append([
             send(latp.at[m, rows(j, SUB)], latr.at[k, m], at_tensor(j)) for k, j in enumerate(tens)
-        ]
+        ])
+    fw.append(dq_forward(1))
 
     for m in range(2):
         for q in range(4):
@@ -180,22 +197,22 @@
                 elif e == 0:
                     htl[q, 0:64, m * TOK:(m + 1) * TOK] = hid[m, :, base:base + 128].T[64:128]
     hall[d] = htl[d]
-    fw0 = dq_forward(0, out0)
-
-    for c in lt:
-        c.wait_recv()
-
-    def total(part, recv):
-        x = part[:, rows(t, SUB)].astype(F32)
+
+    def total(part, recv, m):
+        v = part[m, rows(t, SUB)].astype(F32)
         for k in range(3):
-            x = x + recv[k].astype(F32)
-        return x.reshape(2 * SUB, QL)
-
-    lat = total(latp, latr)
+            v = v + recv[k, m].astype(F32)
+        return v
+
     g = gain[...].astype(F32)
-    inv = lax.rsqrt(jnp.mean(lat * lat, axis=-1, keepdims=True) + EPSILON)
-    nz[t] = (lat * inv * g).astype(BF16)
-    an = [send(nz.at[t], nz.at[t], at_tensor(j)) for j in tens]
+    an = []
+    for n, m in enumerate((core, 1 - core)):
+        for c in lt[n]:
+            c.wait_recv()
+        lat = total(latp, latr, m)
+        inv = lax.rsqrt(jnp.mean(lat * lat, axis=-1, keepdims=True) + EPSILON)
+        nz[t, m] = (lat * inv * g).astype(BF16)
+        an.append([send(nz.at[t, m], nz.at[t, m], at_tensor(j)) for j in tens])
 
     def hi_lo(v):
         high = v.astype(BF16)
@@ -206,36 +223,43 @@
 
     for c in gn:
         c.wait_recv()
-    gnrm = total(gnp, gnr)
-    scaled = gnrm * g
-    glat = inv * scaled - lat * (inv * inv * inv) * jnp.mean(scaled * lat, axis=-1, keepdims=True)
-    gz[t, 0:2 * SUB] = glat.astype(BF16)
-    gz[t, 2 * SUB:2 * SUB + 16] = hi_lo(jnp.sum(gnrm * lat * inv, axis=0, keepdims=True))
-
-    fw1 = dq_forward(1, out1)
-
-    for c in an:
-        c.wait_recv()
-    ag = [send(gz.at[t], gz.at[t], at_tensor(j)) for j in tens]
+    part = jnp.zeros((1, QL), F32)
     for m in range(2):
-        full = jnp.concatenate([nz[k, m * SUB:(m + 1) * SUB] for k in range(4)], axis=0)
+        lat = total(latp, latr, m)
+        inv = lax.rsqrt(jnp.mean(lat * lat, axis=-1, keepdims=True) + EPSILON)
+        gnrm = total(gnp, gnr, m)
+        scaled = gnrm * g
+        back_mean = jnp.mean(scaled * lat, axis=-1, keepdims=True)
+        gz[t, m * SUB:(m + 1) * SUB] = (
+            inv * scaled - lat * (inv * inv * inv) * back_mean
+        ).astype(BF16)
+        part = part + jnp.sum(gnrm * lat * inv, axis=0, keepdims=True)
+    gz[t, 2 * SUB:2 * SUB + 16] = hi_lo(part)
+
+    for n, m in enumerate((core, 1 - core)):
+        for c in an[n]:
+            c.wait_recv()
+        if n == 1:
+            ag = [send(gz.at[t], gz.at[t], at_tensor(j)) for j in tens]
+        full = jnp.concatenate([nz[k, m] for k in range(4)], axis=0)
+        lanes = pl.ds(pl.multiple_of(m * TOK, TOK), TOK)
         for q in range(QL // 64):
             if q % 2 == 0:
                 tr = full[:, q * 64:q * 64 + 128].T
             dst, off = q * 64 // USH, q * 64 % USH
-            ntl[dst, off:off + 64, m * TOK:(m + 1) * TOK] = tr[(q % 2) * 64:(q % 2) * 64 + 64]
+            ntl[dst, off:off + 64, lanes] = tr[(q % 2) * 64:(q % 2) * 64 + 64]
     nt = [send(ntl.at[j], nall.at[d], at_dp(j)) for j in dps]
     nall[d] = ntl[d]
-    ht = [send(htl.at[j], hall.at[d], at_dp(j)) for j in dps]
+    fw.append(dq_forward(2))
+    fw.append(dq_forward(3))
 
     for c in nt:
         c.wait_recv()
     ups = []
-    for n in range(UCH):
-        if n % (UCH // 2) == 0:
-            h = n // (UCH // 2)
-            for c in ((out0, out1)[h][2], (out0, out1)[h][3]) + (fw0, fw1)[h]:
-                c.wait_recv()
+
+    def grad_up(n):
+        for c in (out[n][2], out[n][3]) + fw[n]:
+            c.wait_recv()
         acc = jnp.zeros((USH, UW), F32)
         for k in range(4):
             acc = acc + jnp.dot(
@@ -245,6 +269,9 @@
         ups.append(send(ubuf.at[n], u_rec.at[n], mirror))
         load(ubuf.at[n], u_own.at[n])
 
+    grad_up(0)
+    grad_up(1)
+
     for c in ag:
         c.wait_recv()
     for n in range(DCH):
@@ -256,13 +283,25 @@
 
     def gain_rows(parts):
         v = jnp.zeros((1, QL), F32)
-        for x in parts:
-            v = v + jnp.sum(x.astype(F32), axis=0, keepdims=True)
+        for p in parts:
+            v = v + jnp.sum(p.astype(F32), axis=0, keepdims=True)
         return v
 
     gg[d] = hi_lo(gain_rows([gz[k, 2 * SUB:2 * SUB + 16] for k in range(4)]))
+    ga = [[
+        send(gl.at[n, d, r], gl.at[n, d, r], at_dp(j))
+        for r, j in ((lo, up), (hi, dn), (hi, up), (lo, dn))
+    ] for n in range(DCH)]
     gs = [send(gg.at[d], gg.at[d], at_dp(j)) for j in dps]
-    ga = [[send(gl.at[n, d], gl.at[n, d], at_dp(j)) for j in dps] for n in range(DCH)]
+    ht = [send(htl.at[j], hall.at[d], at_dp(j)) for j in dps]
+    grad_up(2)
+    grad_up(3)
+
+    for n in range(DCH):
+        ga[n][0].wait_recv()
+        ga[n].append(send(gl.at[n, dn, lo], gl.at[n, dn, lo], at_dp(up)))
+        ga[n][1].wait_recv()
+        ga[n].append(send(gl.at[n, up, hi], gl.at[n, up, hi], at_dp(dn)))
 
     for c in gs:
         c.wait_recv()
@@ -277,7 +316,7 @@
     for c in ht:
         c.wait_recv()
     for n in range(DCH):
-        for c in ga[n]:
+        for c in ga[n][2:]:
             c.wait_recv()
         acc = jnp.zeros((DSH, DW), F32)
         for k in range(4):
@@ -304,10 +343,11 @@
     anywhere = pl.BlockSpec(memory_space=pl.ANY)
     vmem = pl.BlockSpec(memory_space=pltpu.VMEM)
     shapes = [
-        (2, TOK, DM), (TOK, DM), (TOK, DM), (CH, BLK, DM), (CH, BLK, DM), (TOK, DM), (2, TOK, DM),
+        (2, TOK, DM), (TOK, DM), (TOK, DM), (2, 4, BLK, DM), (2, 4, BLK, DM), (2, BLK, DM),
+        (2, BLK, DM), (2, 4, BLK, DM), (TOK, DM), (2, TOK, DM),
         (4, 2 * TOK, HQ), (DM, QL), (QL, HQ),
         (2, TOK, QL), (3, 2, SUB, QL), (2, TOK, QL), (3, 2, SUB, QL),
-        (4, 2 * SUB, QL), (4, 2 * SUB + 16, QL),
+        (4, 2, SUB, QL), (4, 2 * SUB + 16, QL),
         (4, USH, 2 * TOK), (4, USH, 2 * TOK), (DCH, 4, 2 * TOK, DW), (4, 16, QL),
         (4, DSH, 2 * TOK), (4, DSH, 2 * TOK),
         (UCH, USH, UW), (DCH, DSH, DW), (16, USH),
@@ -318,7 +358,7 @@
         out_shape=[jax.ShapeDtypeStruct(x, BF16) for x in halves],
         in_specs=[anywhere, anywhere, anywhere, vmem, anywhere, anywhere, anywhere],
         out_specs=[anywhere] * 6,
-        scratch_shapes=[pltpu.VMEM(x, BF16) for x in shapes] + [
+        scratch_shapes=[pltpu.VMEM(x, F32 if i == 4 else BF16) for i, x in enumerate(shapes)] + [
             pltpu.SemaphoreType.DMA((16,)),
             pltpu.SemaphoreType.DMA((NCOPY,)),
             pltpu.SemaphoreType.DMA((NCOPY,)),

time: 118 us -> 114 us (0.966)
  Pallas kernels: 117 us -> 113 us
    pallas_call x1, Pallas kernels: 113 us -> 109 us  [local(): pl.pallas_call(kernel, out_shape=[jax.ShapeDtypeStruct(x, BF16) for x in...]
where the time goes in v3:
time: 114 us
  Pallas kernels  113 us (99%)
    pallas_call x1, Pallas kernels, local(): pl.pallas_call(kernel, out_shape=[jax.ShapeDtypeStruct(x, BF16) for x in...  109 us
    pallas_call x1, Pallas kernels, local(): pl.pallas_call(finish, grid=(4,), out_shape=(jax.ShapeDtypeStruct((DSH, Q...  4.07 us

profile of v3, /device:TPU:1, one launch (start us, length us, event | category | flops | bytes accessed | tf_op | source)
XLA Modules:
  0.0 113.9 jit_solution(2727746683730197784)
XLA Ops:
  0.6 109.2 %sections.1 = (bf16[4,192,768]{2,1,0:T(8,128)(2,1)}, bf16[4,192,768]{2,1,0:T(8,128)(2,1)}, bf16[2,448,384]{2,1,0:T(8,128)(2,1)}, bf16[2,448,384]{2,1,0:T(8,128)(...) custom-call(bf16[128,1792]{1,0:T(8,128)(2,1)} %bitcast.12, bf16[128,1792]{1,0:T(8,128)(2,1)} %bitcast.13, ...), custom_call_target="tpu_custom_call" | custom-call | tf_op jit(solution)/shard_map/sections/pallas_call | solution.py:356
  109.9 4.1 %finish.1 = (bf16[448,768]{1,0:T(8,128)(2,1)}, bf16[1,192]{1,0:T(2,128)(2,1)}, bf16[192,3072]{1,0:T(8,128)(2,1)}) custom-call(bf16[4,192,768]{2,1,0:T(8,128)(2,1)} %get-tuple-element.12.u_own, bf16[4,192,768]{2,1,0:T(8,128)(2,1)} %get-tuple-element.13.u_rec, bf16[2,448,384]{2,1,0:T(8,128)(2,1)} %get-tuple-element.14.d_own, ...), custom_call_target="tpu_custom_call" | custom-call | tf_op jit(solution)/shard_map/finish/pallas_call | solution.py:374

commit v4 on v3

--- a/solution.py
+++ b/solution.py
@@ -22,9 +22,9 @@
 USH = QL // 4
 UCH = 4
 UW = HQ // UCH
-DCH = 2
-DW = QL // DCH
-NCOPY = 96
+DCOLS = ((0, 384), (384, 256), (640, 128))
+NCOPY = 128
+STEPS = 2
 
 
 def rows(i, n):
@@ -68,6 +68,7 @@
     def send(src, dst, to):
         i = counter[0]
         counter[0] += 1
+        assert i < NCOPY
         copy = pltpu.make_async_remote_copy(
             src_ref=src, dst_ref=dst, send_sem=ss.at[i], recv_sem=rs.at[i],
             device_id=to, device_id_type=MESH,
@@ -250,8 +251,6 @@
             ntl[dst, off:off + 64, lanes] = tr[(q % 2) * 64:(q % 2) * 64 + 64]
     nt = [send(ntl.at[j], nall.at[d], at_dp(j)) for j in dps]
     nall[d] = ntl[d]
-    fw.append(dq_forward(2))
-    fw.append(dq_forward(3))
 
     for c in nt:
         c.wait_recv()
@@ -269,17 +268,16 @@
         ups.append(send(ubuf.at[n], u_rec.at[n], mirror))
         load(ubuf.at[n], u_own.at[n])
 
+    fw.append(dq_forward(2))
     grad_up(0)
+    fw.append(dq_forward(3))
     grad_up(1)
 
     for c in ag:
         c.wait_recv()
-    for n in range(DCH):
-        for m in range(2):
-            for k in range(4):
-                gl[n, d, m * TOK + k * SUB:m * TOK + (k + 1) * SUB] = gz[
-                    k, m * SUB:(m + 1) * SUB, n * DW:(n + 1) * DW
-                ]
+    for m in range(2):
+        for k in range(4):
+            gl[d, m * TOK + k * SUB:m * TOK + (k + 1) * SUB] = gz[k, m * SUB:(m + 1) * SUB]
 
     def gain_rows(parts):
         v = jnp.zeros((1, QL), F32)
@@ -288,20 +286,33 @@
         return v
 
     gg[d] = hi_lo(gain_rows([gz[k, 2 * SUB:2 * SUB + 16] for k in range(4)]))
-    ga = [[
-        send(gl.at[n, d, r], gl.at[n, d, r], at_dp(j))
-        for r, j in ((lo, up), (hi, dn), (hi, up), (lo, dn))
-    ] for n in range(DCH)]
+    ga = []
+
+    def cols(n):
+        return pl.ds(*DCOLS[n])
+
+    def gl_out(n):
+        ga.append([
+            send(gl.at[d, r, cols(n)], gl.at[d, r, cols(n)], at_dp(j))
+            for r, j in ((lo, up), (hi, dn), (hi, up), (lo, dn))
+        ])
+
+    gl_out(0)
+    gl_out(1)
     gs = [send(gg.at[d], gg.at[d], at_dp(j)) for j in dps]
     ht = [send(htl.at[j], hall.at[d], at_dp(j)) for j in dps]
     grad_up(2)
     grad_up(3)
 
-    for n in range(DCH):
+    def gl_forward(n):
         ga[n][0].wait_recv()
-        ga[n].append(send(gl.at[n, dn, lo], gl.at[n, dn, lo], at_dp(up)))
+        ga[n].append(send(gl.at[dn, lo, cols(n)], gl.at[dn, lo, cols(n)], at_dp(up)))
         ga[n][1].wait_recv()
-        ga[n].append(send(gl.at[n, up, hi], gl.at[n, up, hi], at_dp(dn)))
+        ga[n].append(send(gl.at[up, hi, cols(n)], gl.at[up, hi, cols(n)], at_dp(dn)))
+
+    gl_forward(0)
+    gl_out(2)
+    gl_forward(1)
 
     for c in gs:
         c.wait_recv()
@@ -315,15 +326,17 @@
 
     for c in ht:
         c.wait_recv()
-    for n in range(DCH):
+    for n in range(len(DCOLS)):
+        if n == 1:
+            gl_forward(2)
         for c in ga[n][2:]:
             c.wait_recv()
-        acc = jnp.zeros((DSH, DW), F32)
+        acc = jnp.zeros((DSH, DCOLS[n][1]), F32)
         for k in range(4):
-            acc = acc + jnp.dot(hall[k], gl[n, k], preferred_element_type=F32)
-        dbuf[n] = acc.astype(BF16)
-        last.append(send(dbuf.at[n], d_rec.at[n], mirror))
-        load(dbuf.at[n], d_own.at[n])
+            acc = acc + jnp.dot(hall[k], gl[k, :, cols(n)], preferred_element_type=F32)
+        dbuf[:, cols(n)] = acc.astype(BF16)
+        last.append(send(dbuf.at[:, cols(n)], d_rec.at[:, cols(n)], mirror))
+        load(dbuf.at[:, cols(n)], d_own.at[:, cols(n)])
 
     for c in ups + last:
         c.wait_recv()
@@ -334,8 +347,10 @@
 
 
 def finish(u_own, u_rec, d_own, d_rec, g_own, g_rec, down, gain, up):
-    up[...] = (u_own[0].astype(F32) + u_rec[0].astype(F32)).astype(BF16)
-    down[...] = (d_own[0].astype(F32) + d_rec[0].astype(F32)).astype(BF16)
+    for n in range(UCH // STEPS):
+        both = u_own[n].astype(F32) + u_rec[n].astype(F32)
+        up[:, n * UW:(n + 1) * UW] = both.astype(BF16)
+    down[...] = (d_own[...].astype(F32) + d_rec[...].astype(F32)).astype(BF16)
     gain[...] = (g_own[0:1].astype(F32) + g_rec[0:1].astype(F32)).astype(BF16)
 
 
@@ -348,11 +363,11 @@
         (4, 2 * TOK, HQ), (DM, QL), (QL, HQ),
         (2, TOK, QL), (3, 2, SUB, QL), (2, TOK, QL), (3, 2, SUB, QL),
         (4, 2, SUB, QL), (4, 2 * SUB + 16, QL),
-        (4, USH, 2 * TOK), (4, USH, 2 * TOK), (DCH, 4, 2 * TOK, DW), (4, 16, QL),
+        (4, USH, 2 * TOK), (4, USH, 2 * TOK), (4, 2 * TOK, QL), (4, 16, QL),
         (4, DSH, 2 * TOK), (4, DSH, 2 * TOK),
-        (UCH, USH, UW), (DCH, DSH, DW), (16, USH),
+        (UCH, USH, UW), (DSH, QL), (16, USH),
     ]
-    halves = [(UCH, USH, UW)] * 2 + [(DCH, DSH, DW)] * 2 + [(16, USH)] * 2
+    halves = [(UCH, USH, UW)] * 2 + [(DSH, QL)] * 2 + [(16, USH)] * 2
     parts = pl.pallas_call(
         kernel,
         out_shape=[jax.ShapeDtypeStruct(x, BF16) for x in halves],
@@ -368,12 +383,12 @@
         ),
         name="sections",
     )(attn_a[0], attn_b[0], w_down[0], q_gain, w_up[0], dq_a[0], dq_b[0])
-    ublock = pl.BlockSpec((1, USH, UW), lambda n: (n, 0, 0))
-    dblock = pl.BlockSpec((1, DSH // 2, DW), lambda n: (n // 2, n % 2, 0))
+    ublock = pl.BlockSpec((UCH // STEPS, USH, UW), lambda n: (n, 0, 0))
+    dblock = pl.BlockSpec((DSH // STEPS, QL), lambda n: (n, 0))
     gblock = pl.BlockSpec((16, USH), lambda n: (0, 0))
     down, gain, up = pl.pallas_call(
         finish,
-        grid=(4,),
+        grid=(STEPS,),
         out_shape=(
             jax.ShapeDtypeStruct((DSH, QL), BF16),
             jax.ShapeDtypeStruct((1, USH), BF16),
@@ -381,9 +396,9 @@
         ),
         in_specs=[ublock, ublock, dblock, dblock, gblock, gblock],
         out_specs=(
-            pl.BlockSpec((DSH // 2, DW), lambda n: (n % 2, n // 2)),
+            dblock,
             pl.BlockSpec((1, USH), lambda n: (0, 0)),
-            pl.BlockSpec((USH, UW), lambda n: (0, n)),
+            pl.BlockSpec((USH, HQ // STEPS), lambda n: (0, n)),
         ),
         compiler_params=pltpu.CompilerParams(vmem_limit_bytes=56 * 2**20),
         name="finish",

time: 114 us -> 111 us (0.974)
  Pallas kernels: 113 us -> 110 us
    pallas_call x1, Pallas kernels: 109 us -> 107 us  [local(): pl.pallas_call(kernel, out_shape=[jax.ShapeDtypeStruct(x, BF16) for x in...]
where the time goes in v4:
time: 111 us; the launch traced here: 110 us
  Pallas kernels  110 us (99%)
    pallas_call x1, Pallas kernels, local(): pl.pallas_call(kernel, out_shape=[jax.ShapeDtypeStruct(x, BF16) for x in...  107 us
    pallas_call x1, Pallas kernels, local(): pl.pallas_call(finish, grid=(STEPS,), out_shape=(jax.ShapeDtypeStruct((DS...  3.14 us

profile of v4, /device:TPU:1, one launch (start us, length us, event | category | flops | bytes accessed | tf_op | source)
XLA Modules:
  0.0 110.3 jit_solution(10759741400518063983)
XLA Ops:
  0.6 106.5 %sections.1 = (bf16[4,192,768]{2,1,0:T(8,128)(2,1)}, bf16[4,192,768]{2,1,0:T(8,128)(2,1)}, bf16[448,768]{1,0:T(8,128)(2,1)}, bf16[448,768]{1,0:T(8,128)(2,1)}, b...) custom-call(bf16[128,1792]{1,0:T(8,128)(2,1)} %bitcast.12, bf16[128,1792]{1,0:T(8,128)(2,1)} %bitcast.13, ...), custom_call_target="tpu_custom_call" | custom-call | tf_op jit(solution)/shard_map/sections/pallas_call | solution.py:371
  107.1 3.1 %finish.1 = (bf16[448,768]{1,0:T(8,128)(2,1)}, bf16[1,192]{1,0:T(2,128)(2,1)}, bf16[192,3072]{1,0:T(8,128)(2,1)}) custom-call(bf16[4,192,768]{2,1,0:T(8,128)(2,1)} %get-tuple-element.12.u_own, bf16[4,192,768]{2,1,0:T(8,128)(2,1)} %get-tuple-element.13.u_rec, bf16[448,768]{1,0:T(8,128)(2,1)} %get-tuple-element.14.d_own, ...), custom_call_target="tpu_custom_call" | custom-call | tf_op jit(solution)/shard_map/finish/pallas_call | solution.py:389

commit v5 on v4

--- a/solution.py
+++ b/solution.py
@@ -35,7 +35,7 @@
     attn_a, attn_b, w_down, gain, w_up, dq_a, dq_b,
     u_own, u_rec, d_own, d_rec, g_own, g_rec,
     att, xin, tot, got, pre, zout, zin, pout, pfx, hid, dq, wd, wu,
-    gnp, gnr, latp, latr, nz, gz, ntl, nall, gl, gg, htl, hall,
+    gnp, gnr, latp, latr, nz, gz, gp, ntl, nall, gl, gg, htl, hall,
     ubuf, dbuf, gbuf,
     lsem, ss, rs,
 ):
@@ -216,11 +216,14 @@
         an.append([send(nz.at[t, m], nz.at[t, m], at_tensor(j)) for j in tens])
 
     def hi_lo(v):
-        high = v.astype(BF16)
-        low = (v - high.astype(F32)).astype(BF16)
-        r = lax.broadcasted_iota(jnp.int32, (16, QL), 0)
-        both = jnp.where(r == 0, high.astype(F32), jnp.where(r == 1, low.astype(F32), 0.0))
-        return both.astype(BF16)
+        high = v.astype(BF16).astype(F32)
+        return jnp.concatenate([high, v - high, jnp.zeros((4, 128), F32)], axis=0).astype(BF16)
+
+    def gain_rows(parts):
+        v = jnp.zeros((16, 128), F32)
+        for p in parts:
+            v = v + p.astype(F32)
+        return v[0:6] + v[6:12]
 
     for c in gn:
         c.wait_recv()
@@ -235,13 +238,16 @@
             inv * scaled - lat * (inv * inv * inv) * back_mean
         ).astype(BF16)
         part = part + jnp.sum(gnrm * lat * inv, axis=0, keepdims=True)
-    gz[t, 2 * SUB:2 * SUB + 16] = hi_lo(part)
+    gp[t] = hi_lo(
+        jnp.concatenate([part[:, q * 128:(q + 1) * 128] for q in range(QL // 128)], axis=0)
+    )
 
     for n, m in enumerate((core, 1 - core)):
         for c in an[n]:
             c.wait_recv()
         if n == 1:
             ag = [send(gz.at[t], gz.at[t], at_tensor(j)) for j in tens]
+            gq = [send(gp.at[t], gp.at[t], at_tensor(j)) for j in tens]
         full = jnp.concatenate([nz[k, m] for k in range(4)], axis=0)
         lanes = pl.ds(pl.multiple_of(m * TOK, TOK), TOK)
         for q in range(QL // 64):
@@ -279,13 +285,9 @@
         for k in range(4):
             gl[d, m * TOK + k * SUB:m * TOK + (k + 1) * SUB] = gz[k, m * SUB:(m + 1) * SUB]
 
-    def gain_rows(parts):
-        v = jnp.zeros((1, QL), F32)
-        for p in parts:
-            v = v + jnp.sum(p.astype(F32), axis=0, keepdims=True)
-        return v
-
-    gg[d] = hi_lo(gain_rows([gz[k, 2 * SUB:2 * SUB + 16] for k in range(4)]))
+    for c in gq:
+        c.wait_recv()
+    gg[d] = hi_lo(gain_rows([gp[k] for k in range(4)]))
     ga = []
 
     def cols(n):
@@ -317,6 +319,7 @@
     for c in gs:
         c.wait_recv()
     sums = gain_rows([gg[k] for k in range(4)])
+    sums = jnp.concatenate([sums[q:q + 1] for q in range(QL // 128)], axis=1)
     pick = sums[:, 0:USH]
     for q in range(1, 4):
         pick = jnp.where(d == q, sums[:, q * USH:(q + 1) * USH], pick)
@@ -362,8 +365,8 @@
         (2, BLK, DM), (2, 4, BLK, DM), (TOK, DM), (2, TOK, DM),
         (4, 2 * TOK, HQ), (DM, QL), (QL, HQ),
         (2, TOK, QL), (3, 2, SUB, QL), (2, TOK, QL), (3, 2, SUB, QL),
-        (4, 2, SUB, QL), (4, 2 * SUB + 16, QL),
-        (4, USH, 2 * TOK), (4, USH, 2 * TOK), (4, 2 * TOK, QL), (4, 16, QL),
+        (4, 2, SUB, QL), (4, 2 * SUB, QL), (4, 16, 128),
+        (4, USH, 2 * TOK), (4, USH, 2 * TOK), (4, 2 * TOK, QL), (4, 16, 128),
         (4, DSH, 2 * TOK), (4, DSH, 2 * TOK),
         (UCH, USH, UW), (DSH, QL), (16, USH),
     ]

time: 111 us -> 110 us (level)
  no operation moved by 1% of the time
where the time goes in v5:
time: 110 us; the launch traced here: 109 us
  Pallas kernels  109 us (99%)
    pallas_call x1, Pallas kernels, local(): pl.pallas_call(kernel, out_shape=[jax.ShapeDtypeStruct(x, BF16) for x in...  106 us
    pallas_call x1, Pallas kernels, local(): pl.pallas_call(finish, grid=(STEPS,), out_shape=(jax.ShapeDtypeStruct((DS...  3.14 us

profile of v5, /device:TPU:1, one launch (start us, length us, event | category | flops | bytes accessed | tf_op | source)
XLA Modules:
  0.0 109.4 jit_solution(15244096691447663706)
XLA Ops:
  0.6 105.6 %sections.1 = (bf16[4,192,768]{2,1,0:T(8,128)(2,1)}, bf16[4,192,768]{2,1,0:T(8,128)(2,1)}, bf16[448,768]{1,0:T(8,128)(2,1)}, bf16[448,768]{1,0:T(8,128)(2,1)}, b...) custom-call(bf16[128,1792]{1,0:T(8,128)(2,1)} %bitcast.12, bf16[128,1792]{1,0:T(8,128)(2,1)} %bitcast.13, ...), custom_call_target="tpu_custom_call" | custom-call | tf_op jit(solution)/shard_map/sections/pallas_call | solution.py:374
  106.3 3.1 %finish.1 = (bf16[448,768]{1,0:T(8,128)(2,1)}, bf16[1,192]{1,0:T(2,128)(2,1)}, bf16[192,3072]{1,0:T(8,128)(2,1)}) custom-call(bf16[4,192,768]{2,1,0:T(8,128)(2,1)} %get-tuple-element.12.u_own, bf16[4,192,768]{2,1,0:T(8,128)(2,1)} %get-tuple-element.13.u_rec, bf16[448,768]{1,0:T(8,128)(2,1)} %get-tuple-element.14.d_own, ...), custom_call_target="tpu_custom_call" | custom-call | tf_op jit(solution)/shard_map/finish/pallas_call | solution.py:392

commit v6 on v5

--- a/solution.py
+++ b/solution.py
@@ -33,10 +33,10 @@
 
 def kernel(
     attn_a, attn_b, w_down, gain, w_up, dq_a, dq_b,
-    u_own, u_rec, d_own, d_rec, g_own, g_rec,
+    u_sum, d_own, d_rec, g_own, g_rec,
     att, xin, tot, got, pre, zout, zin, pout, pfx, hid, dq, wd, wu,
     gnp, gnr, latp, latr, nz, gz, gp, ntl, nall, gl, gg, htl, hall,
-    ubuf, dbuf, gbuf,
+    ubuf, urec, usum, dbuf, gbuf,
     lsem, ss, rs,
 ):
     s, t, d = lax.axis_index("section"), lax.axis_index("tensor"), lax.axis_index("dp")
@@ -271,8 +271,7 @@
                 nall[k], dq[k, :, n * UW:(n + 1) * UW], preferred_element_type=F32
             )
         ubuf[n] = acc.astype(BF16)
-        ups.append(send(ubuf.at[n], u_rec.at[n], mirror))
-        load(ubuf.at[n], u_own.at[n])
+        ups.append(send(ubuf.at[n], urec.at[n], mirror))
 
     fw.append(dq_forward(2))
     grad_up(0)
@@ -341,7 +340,11 @@
         last.append(send(dbuf.at[:, cols(n)], d_rec.at[:, cols(n)], mirror))
         load(dbuf.at[:, cols(n)], d_own.at[:, cols(n)])
 
-    for c in ups + last:
+    for n in range(UCH):
+        ups[n].wait_recv()
+        usum[n] = (ubuf[n].astype(F32) + urec[n].astype(F32)).astype(BF16)
+        load(usum.at[n], u_sum.at[n])
+    for c in last:
         c.wait_recv()
     for c in loads[6:]:
         c.wait()
@@ -349,10 +352,9 @@
         c.wait_send()
 
 
-def finish(u_own, u_rec, d_own, d_rec, g_own, g_rec, down, gain, up):
+def finish(u_sum, d_own, d_rec, g_own, g_rec, down, gain, up):
     for n in range(UCH // STEPS):
-        both = u_own[n].astype(F32) + u_rec[n].astype(F32)
-        up[:, n * UW:(n + 1) * UW] = both.astype(BF16)
+        up[:, n * UW:(n + 1) * UW] = u_sum[n]
     down[...] = (d_own[...].astype(F32) + d_rec[...].astype(F32)).astype(BF16)
     gain[...] = (g_own[0:1].astype(F32) + g_rec[0:1].astype(F32)).astype(BF16)
 
@@ -368,14 +370,14 @@
         (4, 2, SUB, QL), (4, 2 * SUB, QL), (4, 16, 128),
         (4, USH, 2 * TOK), (4, USH, 2 * TOK), (4, 2 * TOK, QL), (4, 16, 128),
         (4, DSH, 2 * TOK), (4, DSH, 2 * TOK),
-        (UCH, USH, UW), (DSH, QL), (16, USH),
+        (UCH, USH, UW), (UCH, USH, UW), (UCH, USH, UW), (DSH, QL), (16, USH),
     ]
-    halves = [(UCH, USH, UW)] * 2 + [(DSH, QL)] * 2 + [(16, USH)] * 2
+    halves = [(UCH, USH, UW)] + [(DSH, QL)] * 2 + [(16, USH)] * 2
     parts = pl.pallas_call(
         kernel,
         out_shape=[jax.ShapeDtypeStruct(x, BF16) for x in halves],
         in_specs=[anywhere, anywhere, anywhere, vmem, anywhere, anywhere, anywhere],
-        out_specs=[anywhere] * 6,
+        out_specs=[anywhere] * 5,
         scratch_shapes=[pltpu.VMEM(x, F32 if i == 4 else BF16) for i, x in enumerate(shapes)] + [
             pltpu.SemaphoreType.DMA((16,)),
             pltpu.SemaphoreType.DMA((NCOPY,)),
@@ -397,7 +399,7 @@
             jax.ShapeDtypeStruct((1, USH), BF16),
             jax.ShapeDtypeStruct((USH, HQ), BF16),
         ),
-        in_specs=[ublock, ublock, dblock, dblock, gblock, gblock],
+        in_specs=[ublock, dblock, dblock, gblock, gblock],
         out_specs=(
             dblock,
             pl.BlockSpec((1, USH), lambda n: (0, 0)),

time: 110 us -> 110 us (level)
  no operation moved by 1% of the time
where the time goes in v6:
time: 110 us; the launch traced here: 109 us
  Pallas kernels  108 us (98%)
    pallas_call x1, Pallas kernels, local(): pl.pallas_call(kernel, out_shape=[jax.ShapeDtypeStruct(x, BF16) for x in...  106 us
    pallas_call x1, Pallas kernels, local(): pl.pallas_call(finish, grid=(STEPS,), out_shape=(jax.ShapeDtypeStruct((DS...  2.7 us

profile of v6, /device:TPU:1, one launch (start us, length us, event | category | flops | bytes accessed | tf_op | source)
XLA Modules:
  0.0 108.9 jit_solution(13397772906427265921)
XLA Ops:
  0.6 105.5 %sections.1 = (bf16[4,192,768]{2,1,0:T(8,128)(2,1)}, bf16[448,768]{1,0:T(8,128)(2,1)}, bf16[448,768]{1,0:T(8,128)(2,1)}, bf16[16,192]{1,0:T(8,128)(2,1)}, bf16[16,192]{1,0:T(8,128)(2,1)}) custom-call(bf16[128,1792]{1,0:T(8,128)(2,1)} %bitcast.12, bf16[128,1792]{1,0:T(8,128)(2,1)} %bitcast.13, bf16[1792,768]{1,0:T(8,128)(2,1)} %bitcast.9, ...), custom_call_target="tpu_custom_call" | custom-call | tf_op jit(solution)/shard_map/sections/pallas_call | solution.py:376
  106.2 2.7 %finish.1 = (bf16[448,768]{1,0:T(8,128)(2,1)}, bf16[1,192]{1,0:T(2,128)(2,1)}, bf16[192,3072]{1,0:T(8,128)(2,1)}) custom-call(bf16[4,192,768]{2,1,0:T(8,128)(2,1)} %get-tuple-element.11.u_sum, bf16[448,768]{1,0:T(8,128)(2,1)} %get-tuple-element.12.d_own, bf16[448,768]{1,0:T(8,128)(2,1)} %get-tuple-element.13.d_rec, bf16[16,192]{1,0:T(8,128)(2,1)} %get-tuple-element.14.g_own, ...), custom_call_target="tpu_custom_call" | custom-call | tf_op jit(solution)/shard_map/finish/pallas_call | solution.py:394
